TPU v7x, 256 devices: a whole 4x4x8 slice. The times are simulated.
256 devices in a mesh: stream: 32 (over x, z), vert: 8 (over y, core).
Axes of the slice: x: 4, y: 4, z: 8, core: 2. Of those that a mesh axis runs over, the one named last changes fastest.
Arguments:
- base_flow: float32 [3, 512, 128, 256], P(None, 'stream', 'vert'), may hold values from -6 to 6
- adjoint_velocity: float32 [3, 512, 128, 256], P(None, 'stream', 'vert'), may hold values from -6 to 6
- reaction: float32 [512, 128, 256], P('stream', 'vert'), may hold values from 0.2 to 20
Outputs:
- advanced_velocity: float32 [3, 512, 128, 256], P(None, 'stream', 'vert')
- pressure: float32 [512, 128, 256], P('stream', 'vert')
All inputs are finite; a program needn't handle non-finite values.
Results may differ from a plain program's by a relative error of at most 0.00014.
Values sent between devices are 32-bit elements; how exact they have to be, the bound alone decides.
A program may use at most 64 MiB of HBM per device.

v0:
```python
import jax
import jax.numpy as jnp
import numpy as np
from jax import lax
from jax.sharding import PartitionSpec as P

ITERS = 3


time_step = 0.05


def extended(array, sides, width):
    for axis, dim in sides:
        devices, length = (lax.axis_size(axis), array.shape[dim])
        up = [(i, (i + 1) % devices) for i in range(devices - 1)]
        down = [(j, i) for i, j in up]
        last = lax.slice_in_dim(array, length - width, length, axis=dim)
        first = lax.slice_in_dim(array, 0, width, axis=dim)
        before = lax.ppermute(last, axis, up)
        after = lax.ppermute(first, axis, down)
        array = jnp.concatenate([before, array, after], axis=dim)
    return array


def gll_tables():
    degree = 7
    inner_nodes = np.array([0.8717401485096066, 0.5917001814331423, 0.2092992179024789])
    points_ref = np.concatenate([[-1.0], -inner_nodes, inner_nodes[::-1], [1.0]])
    previous = np.ones(8)
    current = points_ref.copy()
    for order_now in range(1, degree):
        following = ((2 * order_now + 1) * points_ref * current - order_now * previous) / (
            order_now + 1
        )
        previous = current
        current = following
    quadrature = 2.0 / (degree * (degree + 1) * current**2)
    derivative_table = np.zeros((8, 8))
    for i in range(8):
        for j in range(8):
            if i != j:
                derivative_table[i, j] = current[i] / (current[j] * (points_ref[i] - points_ref[j]))
    derivative_table[0, 0] = -degree * (degree + 1) / 4.0
    derivative_table[7, 7] = degree * (degree + 1) / 4.0
    return (derivative_table, quadrature)


def derive(volume, operator_table, which_axis):
    components, rows_x, rows_y, rows_z = volume.shape
    if which_axis == 1:
        blocks = volume.reshape(components, rows_x // 8, 8, rows_y * rows_z)
        result = jnp.einsum(
            "ab,cebr->cear", operator_table, blocks, precision=lax.Precision.HIGHEST
        )
    elif which_axis == 2:
        blocks = volume.reshape(components * rows_x, rows_y // 8, 8, rows_z)
        result = jnp.einsum(
            "ab,mebz->meaz", operator_table, blocks, precision=lax.Precision.HIGHEST
        )
    else:
        band_matrix = jnp.kron(jnp.eye(16, dtype=operator_table.dtype), operator_table.T)
        result = jnp.dot(volume.reshape(-1, 128), band_matrix, precision=lax.Precision.HIGHEST)
    return result.reshape(volume.shape)


def fold_rim(padded, which_axis):
    length = padded.shape[which_axis] - 2
    centre = lax.slice_in_dim(padded, 1, length + 1, axis=which_axis)
    upper_side = lax.slice_in_dim(padded, 2, length + 2, axis=which_axis)
    lower_side = lax.slice_in_dim(padded, 0, length, axis=which_axis)
    position = lax.broadcasted_iota(jnp.int32, centre.shape, which_axis) % 8
    return (
        centre
        + jnp.where(position == 7, upper_side, 0.0)
        + jnp.where(position == 0, lower_side, 0.0)
    )


def fold_span(volume):
    position = lax.broadcasted_iota(jnp.int32, volume.shape, 3) % 8
    upper_side = jnp.roll(volume, -1, axis=3)
    lower_side = jnp.roll(volume, 1, axis=3)
    return (
        volume
        + jnp.where(position == 7, upper_side, 0.0)
        + jnp.where(position == 0, lower_side, 0.0)
    )


def assemble(volume):
    padded = extended(volume, (("stream", 1),), 1)
    across = fold_rim(padded, 1)
    padded = extended(across, (("vert", 2),), 1)
    across = fold_rim(padded, 2)
    return fold_span(across)


def multiplicity(rows, offset, summed_rows):
    position = jnp.arange(rows, dtype=jnp.int32)
    global_row = offset + position
    shared = (position % 8 == 7) & (global_row < summed_rows - 1) | (position % 8 == 0) & (
        global_row > 0
    )
    return 1.0 + shared.astype(jnp.float32)


def local_operator(volume, derivative_table, weights, reaction):
    summed = derive(weights * derive(volume, derivative_table, 1), derivative_table.T, 1)
    summed = summed + derive(weights * derive(volume, derivative_table, 2), derivative_table.T, 2)
    summed = summed + derive(weights * derive(volume, derivative_table, 3), derivative_table.T, 3)
    return summed + reaction * weights * volume


def convection(base_flow, adjoint_velocity, derivative_table):
    grad_adjoint = [
        derive(adjoint_velocity, derivative_table, which_axis) for which_axis in (1, 2, 3)
    ]
    grad_base = [derive(base_flow, derivative_table, which_axis) for which_axis in (1, 2, 3)]
    carried = (
        base_flow[0] * grad_adjoint[0]
        + base_flow[1] * grad_adjoint[1]
        + base_flow[2] * grad_adjoint[2]
    )
    turned = jnp.stack([jnp.sum(adjoint_velocity * grad_base[c], axis=0) for c in range(3)])
    return carried - turned


def squares(residual, inverse_mult):
    return lax.psum(jnp.sum(residual * residual * inverse_mult), ("stream", "vert"))


def on_device(base_flow, adjoint_velocity, reaction):
    table_host, quad_host = gll_tables()
    derivative_table = jnp.asarray(table_host, jnp.float32)
    quadrature = jnp.asarray(quad_host, jnp.float32)
    components, rows_x, rows_y, rows_z = adjoint_velocity.shape
    weight_x = jnp.tile(quadrature, rows_x // 8)
    weight_y = jnp.tile(quadrature, rows_y // 8)
    weight_z = jnp.tile(quadrature, rows_z // 8)
    weights = weight_x[:, None, None] * weight_y[None, :, None] * weight_z[None, None, :]
    mult_x = multiplicity(
        rows_x, lax.axis_index("stream") * rows_x, rows_x * lax.axis_size("stream")
    )
    mult_y = multiplicity(rows_y, lax.axis_index("vert") * rows_y, rows_y * lax.axis_size("vert"))
    span_pos = jnp.arange(rows_z, dtype=jnp.int32) % 8
    mult_z = 1.0 + ((span_pos == 7) | (span_pos == 0)).astype(jnp.float32)
    mult_all = mult_x[:, None, None] * mult_y[None, :, None] * mult_z[None, None, :]
    inverse_mult = 1.0 / mult_all
    mass_sum = weights * mult_all
    conv = convection(base_flow, adjoint_velocity, derivative_table)
    advanced = adjoint_velocity + time_step * assemble(weights * conv) / mass_sum
    rhs = derive(weights * advanced[0:1], derivative_table.T, 1)
    rhs = rhs + derive(weights * advanced[1:2], derivative_table.T, 2)
    rhs = rhs + derive(weights * advanced[2:3], derivative_table.T, 3)
    rhs = assemble(rhs)
    pressure = jnp.zeros_like(rhs)
    residual = rhs
    direction = rhs
    norm_now = squares(residual, inverse_mult)
    for iteration in range(ITERS):
        applied = assemble(local_operator(direction, derivative_table, weights, reaction))
        curvature = lax.psum(jnp.sum(direction * applied * inverse_mult), ("stream", "vert"))
        step_size = norm_now / curvature
        pressure = pressure + step_size * direction
        residual = residual - step_size * applied
        if iteration + 1 < ITERS:
            norm_next = squares(residual, inverse_mult)
            direction = residual + norm_next / norm_now * direction
            norm_now = norm_next
    grad_pressure = jnp.concatenate(
        [derive(pressure, derivative_table, which_axis) for which_axis in (1, 2, 3)], axis=0
    )
    result = advanced - assemble(weights * grad_pressure) / mass_sum
    return (result, pressure[0])


def solution(mesh):
    placed = (
        P(None, "stream", "vert", None),
        P(None, "stream", "vert", None),
        P("stream", "vert", None),
    )
    return jax.shard_map(
        on_device,
        mesh=mesh,
        in_specs=placed,
        out_specs=(P(None, "stream", "vert", None), P("stream", "vert", None)),
        check_vma=False,
    )
```

profile of v0, /device:TPU:1, one launch (start us, length us, event | category | flops | bytes accessed | tf_op | source)
XLA Modules:
  0.0 545.0 jit_solution(11514832332793988223)
XLA Ops:
  0.7 2.1 reshape.850
  10.5 2.0 convolution_bitcast_fusion.3
  15.8 1.6 fusion.149
  24.2 1.3 collective-permute-start
  25.5 5.0 collective-permute-start.1
  32.0 5.2 collective-permute-start.2
  37.2 2.1 collective-permute-start.3
  39.4 1.7 mul.547
  47.5 4.6 collective-permute-start.5
  53.2 3.3 collective-permute-start.6
  56.4 3.0 collective-permute-start.7
  67.0 1.3 collective-permute-start.8
  68.3 4.6 collective-permute-start.9
  73.9 2.1 collective-permute-start.10
  76.0 4.2 collective-permute-start.11
  83.0 87.4 %all-reduce = (f32[]{:T(128)}, f32[]{:T(128)}) all-reduce(f32[]{:T(128)} %get-tuple-element.6, f32[]{:T(128)} %get-tuple-element.5), channel_id=1, replica_groups=mesh['stream'=32,'vert'=8] {'stream','vert'}, use_global_device_ids=true, to_apply=%region_4.5 | all-reduce | flops 2 | bytes 16 | tf_op jit(solution)/shard_map/psum | solution.py:130
  173.1 73.5 %psum.44 = f32[]{:T(128)} all-reduce(f32[]{:T(128)} %get-tuple-element.11), channel_id=1, replica_groups=mesh['stream'=32,'vert'=8] {'stream','vert'}, use_global_device_ids=true, to_apply=%region_8.9 | all-reduce | flops 1 | bytes 8 | tf_op jit(solution)/shard_map/psum | solution.py:130
  253.9 1.5 fusion.12
  256.7 4.2 collective-permute-start.13
  261.7 3.7 collective-permute-start.14
  265.4 2.8 collective-permute-start.15
  271.0 77.0 %psum.45 = f32[]{:T(128)} all-reduce(f32[]{:T(128)} %get-tuple-element.9), channel_id=1, replica_groups=mesh['stream'=32,'vert'=8] {'stream','vert'}, use_global_device_ids=true, to_apply=%region_10.11 | all-reduce | flops 1 | bytes 8 | tf_op jit(solution)/shard_map/psum | solution.py:163
  350.7 73.7 %psum.46 = f32[]{:T(128)} all-reduce(f32[]{:T(128)} %multiply_reduce_fusion.2), channel_id=1, replica_groups=mesh['stream'=32,'vert'=8] {'stream','vert'}, use_global_device_ids=true, to_apply=%region_12.13 | all-reduce | flops 1 | bytes 8 | tf_op jit(solution)/shard_map/psum | solution.py:130
  431.0 1.4 fusion.8
  433.8 4.0 collective-permute-start.17
  438.8 3.7 collective-permute-start.18
  442.5 2.7 collective-permute-start.19
  448.0 77.0 %psum.47 = f32[]{:T(128)} all-reduce(f32[]{:T(128)} %fusion.84), channel_id=1, replica_groups=mesh['stream'=32,'vert'=8] {'stream','vert'}, use_global_device_ids=true, to_apply=%region_14.15 | all-reduce | flops 1 | bytes 8 | tf_op jit(solution)/shard_map/psum | solution.py:163
  530.1 4.3 collective-permute-start.21
  535.9 3.4 collective-permute-start.22
  539.3 2.2 collective-permute-start.23
  543.5 1.6 fusion.38
  (329 shorter events, 68.0 us)
Async XLA Ops:
  0.6 22.0 %copy-start.56 = (f32[256]{0:T(256)}, f32[256]{0:T(256)S(1)}, u32[]{:S(2)}) copy-start(f32[256]{0:T(256)S(1)} %fusion.115) | copy-start | bytes 3076
  8.0 14.6 %copy-start.47 = (f32[256]{0:T(256)}, f32[256]{0:T(256)S(1)}, u32[]{:S(2)}) copy-start(f32[256]{0:T(256)S(1)} %mul.507) | copy-start | bytes 3076
  24.2 7.5 %collective-permute-start = (f32[3,1,16,256]{3,2,1,0:T(8,128)S(1)}, f32[3,1,16,256]{3,2,1,0:T(8,128)S(1)}, u32[]{:S(2)}, u32[]{:S(2)}) collective-permute-start(f32[3,1,16,256]{3,2,1,0:T(8,128)S(1)} %get-tuple-element.30), channel_id=1, source_target_pairs={{8,0},{16,8},{24,16},{32,24},{40,32},{48,40},{56,48},{64,56},{72,6... | collective-permute-start | bytes 147464 | tf_op jit(solution)/shard_map/ppermute | solution.py:21
  25.5 6.2 %collective-permute-start.1 = (f32[3,1,16,256]{3,2,1,0:T(8,128)S(1)}, f32[3,1,16,256]{3,2,1,0:T(8,128)S(1)}, u32[]{:S(2)}, u32[]{:S(2)}) collective-permute-start(f32[3,1,16,256]{3,2,1,0:T(8,128)S(1)} %get-tuple-element.31), channel_id=1, source_target_pairs={{0,8},{8,16},{16,24},{24,32},{32,40},{40,48},{48,56},{56,64},{64,7... | collective-permute-start | bytes 147464 | tf_op jit(solution)/shard_map/ppermute | solution.py:20
  30.6 11.3 %copy-start.32 = (s32[16]{0:T(128)}, s32[16]{0:T(128)S(1)}, u32[]{:S(2)}) copy-start(s32[16]{0:T(128)S(1)} %get-tuple-element.73) | copy-start | bytes 196
  30.6 11.3 %copy-start.37 = (s32[16]{0:T(128)}, s32[16]{0:T(128)S(1)}, u32[]{:S(2)}) copy-start(s32[16]{0:T(128)S(1)} %get-tuple-element.74) | copy-start | bytes 196
  31.7 10.2 %copy-start.42 = (pred[16]{0:T(512)(128)(4,1)}, pred[16]{0:T(512)(128)(4,1)S(1)}, u32[]{:S(2)}) copy-start(pred[16]{0:T(512)(128)(4,1)S(1)} %compare_and_fusion.1) | copy-start | bytes 52
  32.0 9.0 %collective-permute-start.2 = (f32[3,16,1,256]{3,2,1,0:T(1,128)S(1)}, f32[3,16,1,256]{3,2,1,0:T(1,128)S(1)}, u32[]{:S(2)}, u32[]{:S(2)}) collective-permute-start(f32[3,16,1,256]{3,2,1,0:T(1,128)S(1)} %get-tuple-element.28), channel_id=1, source_target_pairs={{1,0},{2,1},{3,2},{4,3},{5,4},{6,5},{7,6},{9,8},{10,9},{11,10},{12... | collective-permute-start | bytes 147464 | tf_op jit(solution)/shard_map/ppermute | solution.py:21
  37.2 3.8 collective-permute-start.3
  46.2 5.9 %collective-permute-start.4 = (f32[1,1,16,256]{3,2,1,0:T(8,128)S(1)}, f32[1,1,16,256]{3,2,1,0:T(8,128)S(1)}, u32[]{:S(2)}, u32[]{:S(2)}) collective-permute-start(f32[1,1,16,256]{3,2,1,0:T(8,128)S(1)} %get-tuple-element.65), channel_id=1, source_target_pairs={{8,0},{16,8},{24,16},{32,24},{40,32},{48,40},{56,48},{64,56},{72,6... | collective-permute-start | bytes 49160 | tf_op jit(solution)/shard_map/ppermute | solution.py:21
  47.5 5.4 collective-permute-start.5
  53.2 7.8 %collective-permute-start.6 = (f32[1,16,1,256]{3,2,1,0:T(1,128)S(1)}, f32[1,16,1,256]{3,2,1,0:T(1,128)S(1)}, u32[]{:S(2)}, u32[]{:S(2)}) collective-permute-start(f32[1,16,1,256]{3,2,1,0:T(1,128)S(1)} %get-tuple-element.63), channel_id=1, source_target_pairs={{1,0},{2,1},{3,2},{4,3},{5,4},{6,5},{7,6},{9,8},{10,9},{11,10},{12... | collective-permute-start | bytes 49160 | tf_op jit(solution)/shard_map/ppermute | solution.py:21
  56.4 4.6 collective-permute-start.7
  67.0 6.8 %copy-start.34 = (s32[16]{0:T(128)S(1)}, s32[16]{0:T(128)}, u32[]{:S(2)}) copy-start(s32[16]{0:T(128)} %copy-done.32) | copy-start | bytes 196
  67.0 6.7 %copy-start.39 = (s32[16]{0:T(128)S(1)}, s32[16]{0:T(128)}, u32[]{:S(2)}) copy-start(s32[16]{0:T(128)} %copy-done.37) | copy-start | bytes 196
  67.0 6.7 %copy-start.44 = (pred[16]{0:T(512)(128)(4,1)S(1)}, pred[16]{0:T(512)(128)(4,1)}, u32[]{:S(2)}) copy-start(pred[16]{0:T(512)(128)(4,1)} %copy-done.42) | copy-start | bytes 52
  67.0 5.9 %collective-permute-start.8 = (f32[1,1,16,256]{3,2,1,0:T(8,128)S(1)}, f32[1,1,16,256]{3,2,1,0:T(8,128)S(1)}, u32[]{:S(2)}, u32[]{:S(2)}) collective-permute-start(f32[1,1,16,256]{3,2,1,0:T(8,128)S(1)} %get-tuple-element.57), channel_id=1, source_target_pairs={{8,0},{16,8},{24,16},{32,24},{40,32},{48,40},{56,48},{64,56},{72,6... | collective-permute-start | bytes 49160 | tf_op jit(solution)/shard_map/ppermute | solution.py:21
  68.3 5.4 collective-permute-start.9
  73.9 6.3 %collective-permute-start.10 = (f32[1,16,1,256]{3,2,1,0:T(1,128)S(1)}, f32[1,16,1,256]{3,2,1,0:T(1,128)S(1)}, u32[]{:S(2)}, u32[]{:S(2)}) collective-permute-start(f32[1,16,1,256]{3,2,1,0:T(1,128)S(1)} %get-tuple-element.55), channel_id=1, source_target_pairs={{1,0},{2,1},{3,2},{4,3},{5,4},{6,5},{7,6},{9,8},{10,9},{11,10},{12... | collective-permute-start | bytes 49160 | tf_op jit(solution)/shard_map/ppermute | solution.py:21
  76.0 5.0 collective-permute-start.11
  255.4 5.5 %collective-permute-start.12 = (f32[1,1,16,256]{3,2,1,0:T(8,128)S(1)}, f32[1,1,16,256]{3,2,1,0:T(8,128)S(1)}, u32[]{:S(2)}, u32[]{:S(2)}) collective-permute-start(f32[1,1,16,256]{3,2,1,0:T(8,128)S(1)} %get-tuple-element.49), channel_id=1, source_target_pairs={{8,0},{16,8},{24,16},{32,24},{40,32},{48,40},{56,48},{64,56},{72,6... | collective-permute-start | bytes 49160 | tf_op jit(solution)/shard_map/ppermute | solution.py:21
  256.7 4.8 collective-permute-start.13
  261.7 6.5 %collective-permute-start.14 = (f32[1,16,1,256]{3,2,1,0:T(1,128)S(1)}, f32[1,16,1,256]{3,2,1,0:T(1,128)S(1)}, u32[]{:S(2)}, u32[]{:S(2)}) collective-permute-start(f32[1,16,1,256]{3,2,1,0:T(1,128)S(1)} %get-tuple-element.47), channel_id=1, source_target_pairs={{1,0},{2,1},{3,2},{4,3},{5,4},{6,5},{7,6},{9,8},{10,9},{11,10},{12... | collective-permute-start | bytes 49160 | tf_op jit(solution)/shard_map/ppermute | solution.py:21
  265.4 3.6 collective-permute-start.15
  432.5 5.3 collective-permute-start.16
  433.8 4.8 collective-permute-start.17
  438.8 6.4 %collective-permute-start.18 = (f32[1,16,1,256]{3,2,1,0:T(1,128)S(1)}, f32[1,16,1,256]{3,2,1,0:T(1,128)S(1)}, u32[]{:S(2)}, u32[]{:S(2)}) collective-permute-start(f32[1,16,1,256]{3,2,1,0:T(1,128)S(1)} %get-tuple-element.39), channel_id=1, source_target_pairs={{1,0},{2,1},{3,2},{4,3},{5,4},{6,5},{7,6},{9,8},{10,9},{11,10},{12... | collective-permute-start | bytes 49160 | tf_op jit(solution)/shard_map/ppermute | solution.py:21
  442.5 3.6 collective-permute-start.19
  528.8 5.6 %collective-permute-start.20 = (f32[3,1,16,256]{3,2,1,0:T(8,128)S(1)}, f32[3,1,16,256]{3,2,1,0:T(8,128)S(1)}, u32[]{:S(2)}, u32[]{:S(2)}) collective-permute-start(f32[3,1,16,256]{3,2,1,0:T(8,128)S(1)} %get-tuple-element.22), channel_id=1, source_target_pairs={{8,0},{16,8},{24,16},{32,24},{40,32},{48,40},{56,48},{64,56},{72,6... | collective-permute-start | bytes 147464 | tf_op jit(solution)/shard_map/ppermute | solution.py:21
  530.1 5.5 %collective-permute-start.21 = (f32[3,1,16,256]{3,2,1,0:T(8,128)S(1)}, f32[3,1,16,256]{3,2,1,0:T(8,128)S(1)}, u32[]{:S(2)}, u32[]{:S(2)}) collective-permute-start(f32[3,1,16,256]{3,2,1,0:T(8,128)S(1)} %get-tuple-element.23), channel_id=1, source_target_pairs={{0,8},{8,16},{16,24},{24,32},{32,40},{40,48},{48,56},{56,64},{64,7... | collective-permute-start | bytes 147464 | tf_op jit(solution)/shard_map/ppermute | solution.py:20
  535.9 5.6 %collective-permute-start.22 = (f32[3,16,1,256]{3,2,1,0:T(1,128)S(1)}, f32[3,16,1,256]{3,2,1,0:T(1,128)S(1)}, u32[]{:S(2)}, u32[]{:S(2)}) collective-permute-start(f32[3,16,1,256]{3,2,1,0:T(1,128)S(1)} %get-tuple-element.20), channel_id=1, source_target_pairs={{1,0},{2,1},{3,2},{4,3},{5,4},{6,5},{7,6},{9,8},{10,9},{11,10},{12... | collective-permute-start | bytes 147464 | tf_op jit(solution)/shard_map/ppermute | solution.py:21
  539.3 3.3 collective-permute-start.23
  (78 other events, 124.5 us)
where the time goes:
time: 552 us; the launch traced here: 545 us
  blocking collectives  389 us (70%)
  starting transfers between devices  72.8 us (13%)
  local copies, waits for them, and re-layouts  34.1 us (6%)
  matrix products  19.3 us (3%)
  other arithmetic  13.3 us (2%)
  between operations  8.94 us (2%)
  waiting for transfers between devices  7.98 us (1%)
    psum x3, blocking collectives, squares(): lax.psum(jnp.sum(residual * residual * inverse_mult), ('stream', 'vert'))  235 us
    psum x2, blocking collectives, on_device(): lax.psum(jnp.sum(direction * applied * inverse_mult), ('stream', 'vert'))  154 us
    ppermute x12, starting transfers between devices, extended(): before = lax.ppermute(last, axis, up)  43.6 us
    ppermute x12, starting transfers between devices, extended(): after = lax.ppermute(first, axis, down)  29.2 us
    unnamed x181, local copies, waits for them, and re-layouts  18.8 us
  transfers between devices with their start and end apart: 24, of which 9 were waited for; matrix products, arithmetic and copies ran while one was open for 1% of the time, Pallas kernels for 0%

commit v1 on v0

v1 whole, which is shorter than its diff:
```python
import functools

import jax
import jax.numpy as jnp
import ml_dtypes
import numpy as np
from jax import lax
from jax.experimental import pallas as pl
from jax.experimental.pallas import tpu as pltpu
from jax.sharding import PartitionSpec as P

time_step = 0.05
MESH = pl.DeviceIdType.MESH
F32 = jnp.float32
BF16 = jnp.bfloat16
SIDES = ((1, 0), (-1, 0), (0, 1), (0, -1), (1, 1), (1, -1), (-1, 1), (-1, -1))
FIELDS = (3, 1, 1, 4, 6)


def gll_tables():
    degree = 7
    inner_nodes = np.array([0.8717401485096066, 0.5917001814331423, 0.2092992179024789])
    points_ref = np.concatenate([[-1.0], -inner_nodes, inner_nodes[::-1], [1.0]])
    previous = np.ones(8)
    current = points_ref.copy()
    for order_now in range(1, degree):
        following = ((2 * order_now + 1) * points_ref * current - order_now * previous) / (
            order_now + 1
        )
        previous = current
        current = following
    quadrature = 2.0 / (degree * (degree + 1) * current**2)
    derivative_table = np.zeros((8, 8))
    for i in range(8):
        for j in range(8):
            if i != j:
                derivative_table[i, j] = current[i] / (current[j] * (points_ref[i] - points_ref[j]))
    derivative_table[0, 0] = -degree * (degree + 1) / 4.0
    derivative_table[7, 7] = degree * (degree + 1) / 4.0
    return (derivative_table, quadrature)


def halves(matrix):
    high = matrix.astype(np.float32).astype(ml_dtypes.bfloat16)
    low = (matrix - high.astype(np.float64)).astype(ml_dtypes.bfloat16)
    return np.stack([high, low])


def constants(nx, ny, nz):
    table, quad = gll_tables()
    table = table.astype(np.float32).astype(np.float64)
    quad = quad.astype(np.float32).astype(np.float64)
    turned = table.T * quad[None, :] / quad[:, None]
    stiff = turned @ table
    eye = np.eye

    def along_x(m):
        return np.kron(np.kron(eye(nx // 8), m), eye(ny))

    def along_y(m):
        return np.kron(eye(nx * ny // 8), m)

    def along_z(m):
        return np.kron(eye(nz // 8), m.T)

    weights = (
        np.tile(quad, nx // 8)[:, None, None]
        * np.tile(quad, ny // 8)[None, :, None]
        * np.tile(quad, nz // 8)[None, None, :]
    ).astype(np.float32)
    twice = np.array([2.0, 1, 1, 1, 1, 1, 1, 2.0])
    mult = (
        np.tile(twice, nx // 8)[:, None, None]
        * np.tile(twice, ny // 8)[None, :, None]
        * np.tile(twice, nz // 8)[None, None, :]
    )
    return [
        halves(np.concatenate([along_x(table), along_y(table)], axis=0)),
        halves(along_z(table)),
        halves(np.concatenate([along_x(turned), along_y(turned)], axis=1)),
        halves(along_z(turned)),
        halves(along_x(stiff) + along_y(stiff)),
        halves(along_z(stiff)),
        weights,
        (1.0 / mult).astype(np.float32),
    ]


def split(value):
    high = value.astype(BF16)
    low = (value - high.astype(F32)).astype(BF16)
    return high, low


def dot(a, b):
    return jnp.dot(a, b, preferred_element_type=F32)


def left(matrix, parts):
    high, low = parts
    return dot(matrix[0], high) + dot(matrix[0], low) + dot(matrix[1], high)


def right(parts, matrix):
    high, low = parts
    return dot(high, matrix[0]) + dot(low, matrix[0]) + dot(high, matrix[1])


def kernel(
    n_stream,
    n_vert,
    base_h, adj_h, reac_h, kxy_h, kz_h, cxy_h, cz_h, bxy_h, bz_h, w_h, im_h,
    out_h, pres_h,
    base, adj, reac, kxy, kz, cxy, cz, bxy, bz, wts, imult,
    imass, conv, moved, loc, vec, grads, part3, outbuf, pbuf,
    tiles, red_a, red_b,
    in_sem, out_sem, send_sem, recv_sem, red_send, red_recv,
    *halo,
):
    me_s = lax.axis_index("stream")
    me_v = lax.axis_index("vert")
    nx, ny, nz = reac.shape
    rows = nx * ny

    inputs = [
        (kxy_h, kxy), (kz_h, kz), (adj_h, adj), (base_h, base), (w_h, wts), (im_h, imult),
        (cxy_h, cxy), (cz_h, cz), (bxy_h, bxy), (bz_h, bz), (reac_h, reac),
    ]
    loads = [pltpu.make_async_copy(a, b, in_sem.at[i]) for i, (a, b) in enumerate(inputs)]
    for load in loads:
        load.start()

    def near(ds, dv):
        return (lax.rem(me_s + ds + n_stream, n_stream), lax.rem(me_v + dv + n_vert, n_vert))

    barrier = pltpu.get_barrier_semaphore()
    partners = [near(ds, dv) for ds, dv in SIDES]
    partners += [near(0, k) for k in range(1, n_vert)]
    partners += [near(k, 0) for k in range(1, n_stream)]
    for partner in partners:
        pl.semaphore_signal(barrier, inc=1, device_id=partner, device_id_type=MESH)

    def flat(ref):
        return ref[...].reshape(rows, nz)

    lane = lax.broadcasted_iota(jnp.int32, (ny, nz), 1) % 8
    sub = lax.broadcasted_iota(jnp.int32, (8, nz), 0)
    row = lax.broadcasted_iota(jnp.int32, (ny, nz), 0)

    def fold_store(value, ref):
        for i in range(nx):
            v = value[i * ny:(i + 1) * ny]
            up = pltpu.roll(v, nz - 1, 1)
            down = pltpu.roll(v, 1, 1)
            ref[i] = v + jnp.where(lane == 7, up, 0.0) + jnp.where(lane == 0, down, 0.0)
        both = ref[7] + ref[8]
        ref[7] = both
        ref[8] = both
        both = ref[:, 7:8, :] + ref[:, 8:9, :]
        ref[:, 7:8, :] = both
        ref[:, 8:9, :] = both

    def copies(e, src):
        xs, ys, cs = halo[3 * e:3 * e + 3]
        made = []
        for n, (ds, dv) in enumerate(SIDES):
            if dv == 0:
                a = src.at[:, nx - 1 if ds > 0 else 0]
                b = xs.at[0 if ds > 0 else 1]
            else:
                at = pl.ds(ny - 1 if dv > 0 else 0, 1)
                if ds == 0:
                    a = src.at[:, :, at, :]
                    b = ys.at[0 if dv > 0 else 1].at[:, :, pl.ds(0 if dv > 0 else 7, 1), :]
                else:
                    a = src.at[:, nx - 1 if ds > 0 else 0, at, :]
                    b = cs.at[0 if ds > 0 else 1].at[:, pl.ds(0 if dv > 0 else ny - 1, 1), :]
            made.append(
                pltpu.make_async_remote_copy(
                    src_ref=a, dst_ref=b,
                    send_sem=send_sem.at[e, n], recv_sem=recv_sem.at[e, n],
                    device_id=near(ds, dv), device_id_type=MESH,
                )
            )
        for copy in made:
            copy.start()
        return made

    has_xl = me_s > 0
    has_xh = me_s < n_stream - 1
    has_yl = me_v > 0
    has_yh = me_v < n_vert - 1

    def with_halo(e, f, src, i):
        xs, ys, cs = halo[3 * e:3 * e + 3]
        low = src[f, i, 0:8, :] + jnp.where((sub == 0) & has_yl, ys[0, f, i], 0.0)
        high = src[f, i, ny - 8:ny, :] + jnp.where((sub == 7) & has_yh, ys[1, f, i], 0.0)
        value = jnp.concatenate([low, high], axis=0)
        if i in (0, nx - 1):
            side = 0 if i == 0 else 1
            there = has_xl if i == 0 else has_xh
            known = ((row == 0) & has_yl) | ((row == ny - 1) & has_yh)
            value = value + jnp.where(there, xs[side, f] + jnp.where(known, cs[side, f], 0.0), 0.0)
        return value

    def operate(value, parts):
        return wts[...].reshape(rows, nz) * (
            left(bxy, parts) + right(parts, bz) + flat(reac) * value
        )

    def gradient(parts, k, dst, at):
        w = wts[...].reshape(rows, nz)
        both = left(kxy, parts)
        fold_store(w * both[:rows], dst.at[at])
        fold_store(w * both[rows:], dst.at[at + 1])
        fold_store(w * right(parts, kz), dst.at[at + 2])

    def to_row(value, slot):
        s = value.reshape(rows // 8, 8, nz).sum(axis=0)
        s = s[:, :128] + s[:, 128:]
        tiles[0, slot:slot + 1, :] = jnp.sum(s, axis=0, keepdims=True)

    for i in range(4):
        loads[i].wait()
    for c in range(3):
        parts = split(flat(adj.at[c]))
        both = left(kxy, parts)
        conv[c] = (
            flat(base.at[0]) * both[:rows] + flat(base.at[1]) * both[rows:]
            + flat(base.at[2]) * right(parts, kz)
        ).reshape(nx, ny, nz)
    for j in range(3):
        parts = split(flat(base.at[j]))
        a = flat(adj.at[j])
        both = left(kxy, parts)
        conv[0] -= (a * both[:rows]).reshape(nx, ny, nz)
        conv[1] -= (a * both[rows:]).reshape(nx, ny, nz)
        conv[2] -= (a * right(parts, kz)).reshape(nx, ny, nz)
    loads[4].wait()
    for c in range(3):
        fold_store(flat(conv.at[c]) * flat(wts), part3.at[c])
    pl.semaphore_wait(barrier, len(partners))
    sends = [copies(0, part3)]

    loads[5].wait()
    for i in range(nx):
        value = imult[i]
        edge = ((row == 0) & (me_v == 0)) | ((row == ny - 1) & (me_v == n_vert - 1))
        value = value * jnp.where(edge, 2.0, 1.0)
        if i in (0, nx - 1):
            value = value * jnp.where((me_s == 0) if i == 0 else (me_s == n_stream - 1), 2.0, 1.0)
        imult[i] = value
        imass[i] = value / wts[i]
    for i in range(6, 11):
        loads[i].wait()

    for copy in sends[0]:
        copy.wait_recv()
    for c in range(3):
        for i in range(nx):
            moved[c, i] = adj[c, i] + time_step * with_halo(0, c, part3, i) * imass[i]

    pair = jnp.concatenate([flat(moved.at[0]), flat(moved.at[1])], axis=0)
    rhs = left(cxy, split(pair)) + right(split(flat(moved.at[2])), cz)
    fold_store(rhs * flat(wts), loc.at[0].at[0])
    sends.append(copies(1, loc.at[0]))
    for copy in sends[1]:
        copy.wait_recv()
    for i in range(nx):
        vec[0, i] = with_halo(1, 0, loc.at[0], i)

    v = flat(vec.at[0])
    parts = split(v)
    image = operate(v, parts)
    fold_store(image, loc.at[1].at[0])
    sends.append(copies(2, loc.at[1]))
    to_row(v * v * flat(imult), 0)
    to_row(v * image, 1)
    gradient(parts, 0, grads, 1)
    for copy in sends[2]:
        copy.wait_recv()
    for i in range(nx):
        vec[1, i] = with_halo(2, 0, loc.at[1], i)

    v = flat(vec.at[1])
    parts = split(v)
    image = operate(v, parts)
    fold_store(image, grads.at[0])
    sends.append(copies(3, grads))
    to_row(v * v * flat(imult), 2)
    to_row(v * image, 3)
    gradient(parts, 1, outbuf, 0)
    for copy in sends[3]:
        copy.wait_recv()
    for i in range(nx):
        vec[2, i] = with_halo(3, 0, grads, i)

    v = flat(vec.at[2])
    parts = split(v)
    image = operate(v, parts)
    to_row(v * v * flat(imult), 4)
    to_row(v * image, 5)
    tiles[0, 6:8, :] = jnp.zeros((2, 128), F32)

    def spread(src, slots, n, which):
        made = [
            pltpu.make_async_remote_copy(
                src_ref=src, dst_ref=slots.at[k - 1],
                send_sem=red_send.at[which], recv_sem=red_recv.at[which],
                device_id=near(0, k) if which == 0 else near(k, 0), device_id_type=MESH,
            )
            for k in range(1, n)
        ]
        for copy in made:
            copy.start()

    def whole(slots, which):
        return pltpu.make_async_remote_copy(
            src_ref=slots, dst_ref=slots,
            send_sem=red_send.at[which], recv_sem=red_recv.at[which],
            device_id=near(0, 1), device_id_type=MESH,
        )

    spread(tiles.at[0], red_a, n_vert, 0)
    gradient(parts, 2, outbuf, 3)
    sends.append(copies(4, outbuf))
    whole(red_a, 0).wait_recv()
    total = tiles[0]
    for k in range(n_vert - 1):
        total = total + red_a[k]
    tiles[1] = total
    spread(tiles.at[1], red_b, n_stream, 1)

    for d in range(3):
        for i in range(nx):
            conv[d, i] = with_halo(3, 1 + d, grads, i) * imass[i]
    for copy in sends[4]:
        copy.wait_recv()
    for d in range(3):
        for i in range(nx):
            base[d, i] = with_halo(4, d, outbuf, i) * imass[i]
            adj[d, i] = with_halo(4, 3 + d, outbuf, i) * imass[i]

    whole(red_b, 1).wait_recv()
    total = tiles[1]
    for k in range(n_stream - 1):
        total = total + red_b[k]
    m = [jnp.sum(total[k:k + 1], axis=1, keepdims=True) for k in range(6)]
    a0 = m[0] / m[1]
    r1 = a0 * a0 * m[2] - m[0]
    k1 = 1.0 + r1 / m[0]
    p1 = k1 * k1 * m[1] - 2.0 * k1 * a0 * m[2] + a0 * a0 * m[3]
    a1 = r1 / p1
    e1 = -(a0 + a1 * k1)
    e2 = a1 * a0
    r2 = m[0] + 2.0 * e1 * m[1] + (e1 * e1 + 2.0 * e2) * m[2] + 2.0 * e1 * e2 * m[3] + e2 * e2 * m[4]
    b2 = r2 / r1
    f0 = 1.0 + b2 * k1
    f1 = e1 - b2 * a0
    f2 = e2
    p2 = (
        f0 * f0 * m[1] + 2.0 * f0 * f1 * m[2] + (f1 * f1 + 2.0 * f0 * f2) * m[3]
        + 2.0 * f1 * f2 * m[4] + f2 * f2 * m[5]
    )
    a2 = r2 / p2
    c0 = a0 + a1 * k1 + a2 * f0
    c1 = a2 * f1 - a1 * a0
    c2 = a2 * f2

    outs = []
    for i in range(nx):
        pbuf[i] = c0 * vec[0, i] + c1 * vec[1, i] + c2 * vec[2, i]
    outs.append(pltpu.make_async_copy(pbuf, pres_h, out_sem.at[3]))
    outs[-1].start()
    for d in range(3):
        for i in range(nx):
            moved[d, i] = moved[d, i] - (c0 * conv[d, i] + c1 * base[d, i] + c2 * adj[d, i])
        outs.append(pltpu.make_async_copy(moved.at[d], out_h.at[d], out_sem.at[d]))
        outs[-1].start()
    for group in sends:
        for copy in group:
            copy.wait_send()
    whole(red_a, 0).wait_send()
    whole(red_b, 1).wait_send()
    for copy in outs:
        copy.wait()


def on_device(n_stream, n_vert, base_flow, adjoint_velocity, reaction):
    nx, ny, nz = reaction.shape
    consts = constants(nx, ny, nz)
    field = (nx, ny, nz)
    scratch = [
        pltpu.VMEM(base_flow.shape, F32),
        pltpu.VMEM(base_flow.shape, F32),
        pltpu.VMEM(field, F32),
        *[pltpu.VMEM(c.shape, c.dtype) for c in consts],
        pltpu.VMEM(field, F32),
        pltpu.VMEM((3, *field), F32),
        pltpu.VMEM((3, *field), F32),
        pltpu.VMEM((2, 1, *field), F32),
        pltpu.VMEM((3, *field), F32),
        pltpu.VMEM((4, *field), F32),
        pltpu.VMEM((3, *field), F32),
        pltpu.VMEM((6, *field), F32),
        pltpu.VMEM(field, F32),
        pltpu.VMEM((2, 8, 128), F32),
        pltpu.VMEM((n_vert - 1, 8, 128), F32),
        pltpu.VMEM((n_stream - 1, 8, 128), F32),
        pltpu.SemaphoreType.DMA((11,)),
        pltpu.SemaphoreType.DMA((4,)),
        pltpu.SemaphoreType.DMA((5, 8)),
        pltpu.SemaphoreType.DMA((5, 8)),
        pltpu.SemaphoreType.DMA((2,)),
        pltpu.SemaphoreType.DMA((2,)),
    ]
    for count in FIELDS:
        scratch += [
            pltpu.VMEM((2, count, ny, nz), F32),
            pltpu.VMEM((2, count, nx, 8, nz), F32),
            pltpu.VMEM((2, count, ny, nz), F32),
        ]
    return pl.pallas_call(
        functools.partial(kernel, n_stream, n_vert),
        out_shape=(
            jax.ShapeDtypeStruct(base_flow.shape, F32),
            jax.ShapeDtypeStruct(field, F32),
        ),
        in_specs=[pl.BlockSpec(memory_space=pl.ANY)] * 11,
        out_specs=(pl.BlockSpec(memory_space=pl.ANY), pl.BlockSpec(memory_space=pl.ANY)),
        scratch_shapes=scratch,
        compiler_params=pltpu.CompilerParams(
            collective_id=0, has_side_effects=True, vmem_limit_bytes=48 * 1024 * 1024
        ),
    )(base_flow, adjoint_velocity, reaction, *[jnp.asarray(c) for c in consts])


def solution(mesh):
    placed = (
        P(None, "stream", "vert", None),
        P(None, "stream", "vert", None),
        P("stream", "vert", None),
    )
    return jax.shard_map(
        functools.partial(on_device, mesh.shape["stream"], mesh.shape["vert"]),
        mesh=mesh,
        in_specs=placed,
        out_specs=(P(None, "stream", "vert", None), P("stream", "vert", None)),
        check_vma=False,
    )
```

time: 552 us -> 57.7 us (0.10); the launches traced: 545 us -> 57.2 us
  blocking collectives: 389 us -> 0 us
  starting transfers between devices: 72.8 us -> 0 us
  Pallas kernels: 0 us -> 44 us
  local copies, waits for them, and re-layouts: 34.1 us -> 12.6 us
  matrix products: 19.3 us -> 0 us
  other arithmetic: 13.3 us -> 0 us
  between operations: 8.94 us -> 0.66 us
  waiting for transfers between devices: 7.98 us -> 0 us
    psum x5 -> x0, blocking collectives: 389 us -> none  [the longest x3 235 us: squares(): lax.psum(jnp.sum(residual * residual * inverse_mult), ('stream', 'vert'))]
    ppermute x24 -> x0, starting transfers between devices: 72.8 us -> none  [the longest x12 43.6 us: extended(): before = lax.ppermute(last, axis, up)]
    pallas_call x0 -> x1, Pallas kernels: none -> 44 us  [on_device(): pl.pallas_call(functools.partial(kernel, n_stream, n_vert), out_shape=(ja...]
    dot_general x30 -> x0, matrix products: 19.3 us -> none  [the longest x10 9 us: derive(): jnp.einsum('ab,mebz->meaz', operator_table, blocks, precision=lax.Precisi...]
    reshape x16 -> x0, local copies, waits for them, and re-layouts: 9.05 us -> none  [the longest x7 4.57 us: derive(): volume.reshape(-1, 128)]
    ppermute x24 -> x0, waiting for transfers between devices: 7.98 us -> none  [the longest x12 7.95 us: extended(): before = lax.ppermute(last, axis, up)]
    unnamed x181 -> x24, local copies, waits for them, and re-layouts: 18.8 us -> 12.6 us
  transfers between devices with their start and end apart: 24 -> 0, of which waited for: 9 -> 0; matrix products, arithmetic and copies ran while one was open for 1% -> 0% of each run, Pallas kernels for 0% -> 0%
where the time goes in v1:
time: 57.7 us; the launch traced here: 57.2 us
  Pallas kernels  44 us (76%)
  local copies, waits for them, and re-layouts  12.6 us (22%)
  between operations  0.66 us (1%)
    pallas_call x1, Pallas kernels, on_device(): pl.pallas_call(functools.partial(kernel, n_stream, n_vert), out_shape=(ja...  44 us
    unnamed x24, local copies, waits for them, and re-layouts  12.6 us

profile of v1, /device:TPU:1, one launch (start us, length us, event | category | flops | bytes accessed | tf_op | source)
XLA Modules:
  0.0 57.2 jit_solution(1048782113312066281)
XLA Ops:
  0.6 0.0 copy-start
  0.6 1.1 %copy-done = f32[3,16,16,256]{3,2,1,0:T(8,128)S(1)} copy-done((f32[3,16,16,256]{3,2,1,0:T(8,128)S(1)}, f32[3,16,16,256]{3,2,1,0:T(8,128)}, u32[]{:S(2)}) %copy-start) | copy-done | bytes 786456
  1.8 0.0 copy-start.1
  1.8 1.1 %copy-done.1 = f32[3,16,16,256]{3,2,1,0:T(8,128)S(1)} copy-done((f32[3,16,16,256]{3,2,1,0:T(8,128)S(1)}, f32[3,16,16,256]{3,2,1,0:T(8,128)}, u32[]{:S(2)}) %copy-start.1) | copy-done | bytes 786456
  2.9 0.0 copy-start.2
  2.9 1.0 %copy-done.2 = bf16[2,256,512]{2,1,0:T(8,128)(2,1)S(1)} copy-done((bf16[2,256,512]{2,1,0:T(8,128)(2,1)S(1)}, bf16[2,256,512]{2,1,0:T(8,128)(2,1)}, u32[]{:S(2)}) %copy-start.2) | copy-done | bytes 524312
  3.9 0.0 copy-start.3
  3.9 1.0 %copy-done.3 = bf16[2,512,256]{2,1,0:T(8,128)(2,1)S(1)} copy-done((bf16[2,512,256]{2,1,0:T(8,128)(2,1)S(1)}, bf16[2,512,256]{2,1,0:T(8,128)(2,1)}, u32[]{:S(2)}) %copy-start.3) | copy-done | bytes 524312
  5.0 0.0 copy-start.4
  5.0 0.9 %copy-done.4 = f32[16,16,256]{2,1,0:T(8,128)S(1)} copy-done((f32[16,16,256]{2,1,0:T(8,128)S(1)}, f32[16,16,256]{2,1,0:T(8,128)}, u32[]{:S(2)}) %copy-start.4) | copy-done | bytes 262168
  5.9 0.0 copy-start.5
  5.9 0.9 %copy-done.5 = f32[16,16,256]{2,1,0:T(8,128)S(1)} copy-done((f32[16,16,256]{2,1,0:T(8,128)S(1)}, f32[16,16,256]{2,1,0:T(8,128)}, u32[]{:S(2)}) %copy-start.5) | copy-done | bytes 262168
  6.9 0.0 copy-start.6
  6.9 0.9 %copy-done.6 = f32[16,16,256]{2,1,0:T(8,128)S(1)} copy-done((f32[16,16,256]{2,1,0:T(8,128)S(1)}, f32[16,16,256]{2,1,0:T(8,128)}, u32[]{:S(2)}) %copy-start.6) | copy-done | bytes 262168
  7.8 0.0 copy-start.7
  7.8 0.9 %copy-done.7 = bf16[2,256,256]{2,1,0:T(8,128)(2,1)S(1)} copy-done((bf16[2,256,256]{2,1,0:T(8,128)(2,1)S(1)}, bf16[2,256,256]{2,1,0:T(8,128)(2,1)}, u32[]{:S(2)}) %copy-start.7) | copy-done | bytes 262168
  8.8 0.0 copy-start.8
  8.8 0.9 %copy-done.8 = bf16[2,256,256]{2,1,0:T(8,128)(2,1)S(1)} copy-done((bf16[2,256,256]{2,1,0:T(8,128)(2,1)S(1)}, bf16[2,256,256]{2,1,0:T(8,128)(2,1)}, u32[]{:S(2)}) %copy-start.8) | copy-done | bytes 262168
  9.7 0.0 copy-start.9
  9.7 0.9 %copy-done.9 = bf16[2,256,256]{2,1,0:T(8,128)(2,1)S(1)} copy-done((bf16[2,256,256]{2,1,0:T(8,128)(2,1)S(1)}, bf16[2,256,256]{2,1,0:T(8,128)(2,1)}, u32[]{:S(2)}) %copy-start.9) | copy-done | bytes 262168
  10.7 0.0 copy-start.10
  10.7 0.9 %copy-done.10 = bf16[2,256,256]{2,1,0:T(8,128)(2,1)S(1)} copy-done((bf16[2,256,256]{2,1,0:T(8,128)(2,1)S(1)}, bf16[2,256,256]{2,1,0:T(8,128)(2,1)}, u32[]{:S(2)}) %copy-start.10) | copy-done | bytes 262168
  11.6 44.0 %shard_map.122 = (f32[3,16,16,256]{3,2,1,0:T(8,128)S(1)}, f32[16,16,256]{2,1,0:T(8,128)S(1)}) custom-call(f32[3,16,16,256]{3,2,1,0:T(8,128)S(1)} %copy-done, f32[3,16,16,256]{3,2,1,0:T(8,128)S(1)} %copy-done.1, f32[16,16,256]{2,1,0:T(8,128)S(1)} %copy-done.4, bf16[2,512,256]{2,1,0:T(8,128)(2,1)S(1)} %copy-done.3, bf16[2,256,256]{2,1,0:T(8,128)(2,1)S(1)} %copy-done.10, ...), custom_call_target="tpu_custom_call" | custom-call | tf_op jit(solution)/shard_map/pallas_call | solution.py:423
  55.6 0.9 %copy.15 = f32[3,16,16,256]{3,2,1,0:T(8,128)} copy(f32[3,16,16,256]{3,2,1,0:T(8,128)S(1)} %get-tuple-element.4) | data formatting | bytes 1572864
  56.5 0.7 %copy.16 = f32[16,16,256]{2,1,0:T(8,128)} copy(f32[16,16,256]{2,1,0:T(8,128)S(1)} %get-tuple-element.5) | data formatting | bytes 524288
Async XLA Ops:
  0.6 1.1 %copy-start = (f32[3,16,16,256]{3,2,1,0:T(8,128)S(1)}, f32[3,16,16,256]{3,2,1,0:T(8,128)}, u32[]{:S(2)}) copy-start(f32[3,16,16,256]{3,2,1,0:T(8,128)} %base_h.1) | copy-start | bytes 2359300
  1.8 1.1 %copy-start.1 = (f32[3,16,16,256]{3,2,1,0:T(8,128)S(1)}, f32[3,16,16,256]{3,2,1,0:T(8,128)}, u32[]{:S(2)}) copy-start(f32[3,16,16,256]{3,2,1,0:T(8,128)} %adj_h.1) | copy-start | bytes 2359300
  2.9 1.0 %copy-start.2 = (bf16[2,256,512]{2,1,0:T(8,128)(2,1)S(1)}, bf16[2,256,512]{2,1,0:T(8,128)(2,1)}, u32[]{:S(2)}) copy-start(bf16[2,256,512]{2,1,0:T(8,128)(2,1)} %constant.18.clone.cxy_h) | copy-start | bytes 1572868
  3.9 1.0 %copy-start.3 = (bf16[2,512,256]{2,1,0:T(8,128)(2,1)S(1)}, bf16[2,512,256]{2,1,0:T(8,128)(2,1)}, u32[]{:S(2)}) copy-start(bf16[2,512,256]{2,1,0:T(8,128)(2,1)} %constant.16.clone.kxy_h) | copy-start | bytes 1572868
  5.0 0.9 %copy-start.4 = (f32[16,16,256]{2,1,0:T(8,128)S(1)}, f32[16,16,256]{2,1,0:T(8,128)}, u32[]{:S(2)}) copy-start(f32[16,16,256]{2,1,0:T(8,128)} %reac_h.1) | copy-start | bytes 786436
  5.9 0.9 %copy-start.5 = (f32[16,16,256]{2,1,0:T(8,128)S(1)}, f32[16,16,256]{2,1,0:T(8,128)}, u32[]{:S(2)}) copy-start(f32[16,16,256]{2,1,0:T(8,128)} %constant.23.clone.im_h) | copy-start | bytes 786436
  6.9 0.9 %copy-start.6 = (f32[16,16,256]{2,1,0:T(8,128)S(1)}, f32[16,16,256]{2,1,0:T(8,128)}, u32[]{:S(2)}) copy-start(f32[16,16,256]{2,1,0:T(8,128)} %constant.22.clone.w_h) | copy-start | bytes 786436
  7.8 0.9 %copy-start.7 = (bf16[2,256,256]{2,1,0:T(8,128)(2,1)S(1)}, bf16[2,256,256]{2,1,0:T(8,128)(2,1)}, u32[]{:S(2)}) copy-start(bf16[2,256,256]{2,1,0:T(8,128)(2,1)} %constant.21.clone.bz_h) | copy-start | bytes 786436
  8.8 0.9 %copy-start.8 = (bf16[2,256,256]{2,1,0:T(8,128)(2,1)S(1)}, bf16[2,256,256]{2,1,0:T(8,128)(2,1)}, u32[]{:S(2)}) copy-start(bf16[2,256,256]{2,1,0:T(8,128)(2,1)} %constant.20.clone.bxy_h) | copy-start | bytes 786436
  9.7 0.9 %copy-start.9 = (bf16[2,256,256]{2,1,0:T(8,128)(2,1)S(1)}, bf16[2,256,256]{2,1,0:T(8,128)(2,1)}, u32[]{:S(2)}) copy-start(bf16[2,256,256]{2,1,0:T(8,128)(2,1)} %constant.19.clone.cz_h) | copy-start | bytes 786436
  10.7 0.9 %copy-start.10 = (bf16[2,256,256]{2,1,0:T(8,128)(2,1)S(1)}, bf16[2,256,256]{2,1,0:T(8,128)(2,1)}, u32[]{:S(2)}) copy-start(bf16[2,256,256]{2,1,0:T(8,128)(2,1)} %constant.17.clone.kz_h) | copy-start | bytes 786436

commit v2 on v1

--- a/solution.py
+++ b/solution.py
@@ -139,6 +139,19 @@
     partners += [near(k, 0) for k in range(1, n_stream)]
     for partner in partners:
         pl.semaphore_signal(barrier, inc=1, device_id=partner, device_id_type=MESH)
+
+    has_xl = me_s > 0
+    has_xh = me_s < n_stream - 1
+    has_yl = me_v > 0
+    has_yh = me_v < n_vert - 1
+
+    def exists(ds, dv):
+        conditions = []
+        if ds:
+            conditions.append(has_xh if ds > 0 else has_xl)
+        if dv:
+            conditions.append(has_yh if dv > 0 else has_yl)
+        return functools.reduce(jnp.logical_and, conditions)
 
     def flat(ref):
         return ref[...].reshape(rows, nz)
@@ -182,14 +195,17 @@
                     device_id=near(ds, dv), device_id_type=MESH,
                 )
             )
-        for copy in made:
-            copy.start()
+        for copy, (ds, dv) in zip(made, SIDES):
+            pl.when(exists(ds, dv))(copy.start)
         return made
 
-    has_xl = me_s > 0
-    has_xh = me_s < n_stream - 1
-    has_yl = me_v > 0
-    has_yh = me_v < n_vert - 1
+    def arrive(made):
+        for copy, (ds, dv) in zip(made, SIDES):
+            pl.when(exists(-ds, -dv))(copy.wait_recv)
+
+    def leave(made):
+        for copy, (ds, dv) in zip(made, SIDES):
+            pl.when(exists(ds, dv))(copy.wait_send)
 
     def with_halo(e, f, src, i):
         xs, ys, cs = halo[3 * e:3 * e + 3]
@@ -218,7 +234,7 @@
     def to_row(value, slot):
         s = value.reshape(rows // 8, 8, nz).sum(axis=0)
         s = s[:, :128] + s[:, 128:]
-        tiles[0, slot:slot + 1, :] = jnp.sum(s, axis=0, keepdims=True)
+        tiles[slot:slot + 1, :] = jnp.sum(s, axis=0, keepdims=True)
 
     for i in range(4):
         loads[i].wait()
@@ -254,8 +270,7 @@
     for i in range(6, 11):
         loads[i].wait()
 
-    for copy in sends[0]:
-        copy.wait_recv()
+    arrive(sends[0])
     for c in range(3):
         for i in range(nx):
             moved[c, i] = adj[c, i] + time_step * with_halo(0, c, part3, i) * imass[i]
@@ -264,8 +279,7 @@
     rhs = left(cxy, split(pair)) + right(split(flat(moved.at[2])), cz)
     fold_store(rhs * flat(wts), loc.at[0].at[0])
     sends.append(copies(1, loc.at[0]))
-    for copy in sends[1]:
-        copy.wait_recv()
+    arrive(sends[1])
     for i in range(nx):
         vec[0, i] = with_halo(1, 0, loc.at[0], i)
 
@@ -277,8 +291,7 @@
     to_row(v * v * flat(imult), 0)
     to_row(v * image, 1)
     gradient(parts, 0, grads, 1)
-    for copy in sends[2]:
-        copy.wait_recv()
+    arrive(sends[2])
     for i in range(nx):
         vec[1, i] = with_halo(2, 0, loc.at[1], i)
 
@@ -290,8 +303,7 @@
     to_row(v * v * flat(imult), 2)
     to_row(v * image, 3)
     gradient(parts, 1, outbuf, 0)
-    for copy in sends[3]:
-        copy.wait_recv()
+    arrive(sends[3])
     for i in range(nx):
         vec[2, i] = with_halo(3, 0, grads, i)
 
@@ -300,52 +312,49 @@
     image = operate(v, parts)
     to_row(v * v * flat(imult), 4)
     to_row(v * image, 5)
-    tiles[0, 6:8, :] = jnp.zeros((2, 128), F32)
-
-    def spread(src, slots, n, which):
-        made = [
+
+    tiles[6:8, :] = jnp.zeros((2, 128), F32)
+    group = lax.broadcasted_iota(jnp.int32, (8, 128), 1) // 16
+    packed = tiles[...]
+    for shift in (64, 32, 16):
+        packed = packed + pltpu.roll(packed, shift, 1)
+    packed = jnp.where(group == lax.broadcasted_iota(jnp.int32, (8, 128), 0), packed, 0.0)
+    red_a[n_vert - 1:n_vert, :] = jnp.sum(packed, axis=0, keepdims=True)
+
+    def spread(slots, n, which):
+        for k in range(1, n):
             pltpu.make_async_remote_copy(
-                src_ref=src, dst_ref=slots.at[k - 1],
+                src_ref=slots.at[pl.ds(n - 1, 1)], dst_ref=slots.at[pl.ds(k - 1, 1)],
                 send_sem=red_send.at[which], recv_sem=red_recv.at[which],
                 device_id=near(0, k) if which == 0 else near(k, 0), device_id_type=MESH,
-            )
-            for k in range(1, n)
-        ]
-        for copy in made:
-            copy.start()
-
-    def whole(slots, which):
+            ).start()
+
+    def whole(slots, n, which):
         return pltpu.make_async_remote_copy(
-            src_ref=slots, dst_ref=slots,
+            src_ref=slots.at[pl.ds(0, n - 1)], dst_ref=slots.at[pl.ds(0, n - 1)],
             send_sem=red_send.at[which], recv_sem=red_recv.at[which],
             device_id=near(0, 1), device_id_type=MESH,
         )
 
-    spread(tiles.at[0], red_a, n_vert, 0)
+    spread(red_a, n_vert, 0)
     gradient(parts, 2, outbuf, 3)
     sends.append(copies(4, outbuf))
-    whole(red_a, 0).wait_recv()
-    total = tiles[0]
-    for k in range(n_vert - 1):
-        total = total + red_a[k]
-    tiles[1] = total
-    spread(tiles.at[1], red_b, n_stream, 1)
+    whole(red_a, n_vert, 0).wait_recv()
+    red_b[n_stream - 1:n_stream, :] = jnp.sum(red_a[...], axis=0, keepdims=True)
+    spread(red_b, n_stream, 1)
 
     for d in range(3):
         for i in range(nx):
             conv[d, i] = with_halo(3, 1 + d, grads, i) * imass[i]
-    for copy in sends[4]:
-        copy.wait_recv()
+    arrive(sends[4])
     for d in range(3):
         for i in range(nx):
             base[d, i] = with_halo(4, d, outbuf, i) * imass[i]
             adj[d, i] = with_halo(4, 3 + d, outbuf, i) * imass[i]
 
-    whole(red_b, 1).wait_recv()
-    total = tiles[1]
-    for k in range(n_stream - 1):
-        total = total + red_b[k]
-    m = [jnp.sum(total[k:k + 1], axis=1, keepdims=True) for k in range(6)]
+    whole(red_b, n_stream, 1).wait_recv()
+    total = jnp.sum(red_b[...], axis=0, keepdims=True)
+    m = [jnp.sum(jnp.where(group[0:1] == k, total, 0.0), axis=1, keepdims=True) for k in range(6)]
     a0 = m[0] / m[1]
     r1 = a0 * a0 * m[2] - m[0]
     k1 = 1.0 + r1 / m[0]
@@ -377,11 +386,10 @@
             moved[d, i] = moved[d, i] - (c0 * conv[d, i] + c1 * base[d, i] + c2 * adj[d, i])
         outs.append(pltpu.make_async_copy(moved.at[d], out_h.at[d], out_sem.at[d]))
         outs[-1].start()
-    for group in sends:
-        for copy in group:
-            copy.wait_send()
-    whole(red_a, 0).wait_send()
-    whole(red_b, 1).wait_send()
+    for made in sends:
+        leave(made)
+    whole(red_a, n_vert, 0).wait_send()
+    whole(red_b, n_stream, 1).wait_send()
     for copy in outs:
         copy.wait()
 
@@ -404,9 +412,9 @@
         pltpu.VMEM((3, *field), F32),
         pltpu.VMEM((6, *field), F32),
         pltpu.VMEM(field, F32),
-        pltpu.VMEM((2, 8, 128), F32),
-        pltpu.VMEM((n_vert - 1, 8, 128), F32),
-        pltpu.VMEM((n_stream - 1, 8, 128), F32),
+        pltpu.VMEM((8, 128), F32),
+        pltpu.VMEM((n_vert, 128), F32),
+        pltpu.VMEM((n_stream, 128), F32),
         pltpu.SemaphoreType.DMA((11,)),
         pltpu.SemaphoreType.DMA((4,)),
         pltpu.SemaphoreType.DMA((5, 8)),
@@ -430,7 +438,7 @@
         out_specs=(pl.BlockSpec(memory_space=pl.ANY), pl.BlockSpec(memory_space=pl.ANY)),
         scratch_shapes=scratch,
         compiler_params=pltpu.CompilerParams(
-            collective_id=0, has_side_effects=True, vmem_limit_bytes=48 * 1024 * 1024
+            collective_id=0, has_side_effects=True, vmem_limit_bytes=60 * 1024 * 1024
         ),
     )(base_flow, adjoint_velocity, reaction, *[jnp.asarray(c) for c in consts])
 

time: 57.7 us -> 44.6 us (0.77)
  local copies, waits for them, and re-layouts: 12.6 us -> 2.81 us
  Pallas kernels: 44 us -> 41.1 us
    unnamed x24 -> x4, local copies, waits for them, and re-layouts: 12.6 us -> 2.81 us
    pallas_call x1, Pallas kernels: 44 us -> 41.1 us  [on_device(): pl.pallas_call(functools.partial(kernel, n_stream, n_vert), out_shape=(ja...]
where the time goes in v2:
time: 44.6 us; the launch traced here: 44.5 us
  Pallas kernels  41.1 us (92%)
  local copies, waits for them, and re-layouts  2.81 us (6%)
  between operations  0.65 us (1%)
    pallas_call x1, Pallas kernels, on_device(): pl.pallas_call(functools.partial(kernel, n_stream, n_vert), out_shape=(ja...  41.1 us
    unnamed x4, local copies, waits for them, and re-layouts  2.81 us

profile of v2, /device:TPU:1, one launch (start us, length us, event | category | flops | bytes accessed | tf_op | source)
XLA Modules:
  0.0 44.5 jit_solution(5883480806875205919)
XLA Ops:
  0.6 41.1 %shard_map.122 = (f32[3,16,16,256]{3,2,1,0:T(8,128)}, f32[16,16,256]{2,1,0:T(8,128)}) custom-call(f32[3,16,16,256]{3,2,1,0:T(8,128)} %base_h.1, f32[3,16,16,256]{3,2,1,0:T(8,128)} %adj_h.1, f32[16,16,256]{2,1,0:T(8,128)} %reac_h.1, bf16[2,512,256]{2,1,0:T(8,128)(2,1)} %constant.16.clone.kxy_h, bf16[2,256,256]{2,1,0:T(8,128)(2,1)} %constant.17.clone.kz_h, ...), custom_call_target="tpu_custom_call" | custom-call | tf_op jit(solution)/shard_map/pallas_call | solution.py:431
  41.7 0.0 copy-start
  41.7 2.1 %copy.15 = f32[3,16,16,256]{3,2,1,0:T(8,128)} copy(f32[3,16,16,256]{3,2,1,0:T(8,128)} %get-tuple-element.4) | data formatting | bytes 1572864
  43.8 0.0 copy-done
  43.8 0.7 %copy.16 = f32[16,16,256]{2,1,0:T(8,128)} copy(f32[16,16,256]{2,1,0:T(8,128)S(1)} %copy-done) | data formatting | bytes 524288
Async XLA Ops:
  41.7 2.1 %copy-start = (f32[16,16,256]{2,1,0:T(8,128)S(1)}, f32[16,16,256]{2,1,0:T(8,128)}, u32[]{:S(2)}) copy-start(f32[16,16,256]{2,1,0:T(8,128)} %get-tuple-element.5) | copy-start | bytes 786436

commit v3 on v2

--- a/solution.py
+++ b/solution.py
@@ -394,10 +394,20 @@
         copy.wait()
 
 
+def write_out(result, pressure, out_h, pres_h, sems):
+    copies = [pltpu.make_async_copy(result.at[d], out_h.at[d], sems.at[d]) for d in range(3)]
+    copies.append(pltpu.make_async_copy(pressure, pres_h, sems.at[3]))
+    for copy in copies:
+        copy.start()
+    for copy in copies:
+        copy.wait()
+
+
 def on_device(n_stream, n_vert, base_flow, adjoint_velocity, reaction):
     nx, ny, nz = reaction.shape
     consts = constants(nx, ny, nz)
     field = (nx, ny, nz)
+    operands = [base_flow, adjoint_velocity, reaction, *[jnp.asarray(c) for c in consts]]
     scratch = [
         pltpu.VMEM(base_flow.shape, F32),
         pltpu.VMEM(base_flow.shape, F32),
@@ -428,19 +438,30 @@
             pltpu.VMEM((2, count, nx, 8, nz), F32),
             pltpu.VMEM((2, count, ny, nz), F32),
         ]
-    return pl.pallas_call(
+    result, pressure = pl.pallas_call(
         functools.partial(kernel, n_stream, n_vert),
         out_shape=(
-            jax.ShapeDtypeStruct(base_flow.shape, F32),
-            jax.ShapeDtypeStruct(field, F32),
+            pltpu.VMEM(base_flow.shape, F32),
+            pltpu.VMEM(field, F32),
         ),
         in_specs=[pl.BlockSpec(memory_space=pl.ANY)] * 11,
         out_specs=(pl.BlockSpec(memory_space=pl.ANY), pl.BlockSpec(memory_space=pl.ANY)),
         scratch_shapes=scratch,
         compiler_params=pltpu.CompilerParams(
-            collective_id=0, has_side_effects=True, vmem_limit_bytes=60 * 1024 * 1024
+            collective_id=0, has_side_effects=True, vmem_limit_bytes=48 * 1024 * 1024
         ),
-    )(base_flow, adjoint_velocity, reaction, *[jnp.asarray(c) for c in consts])
+    )(*[pltpu.with_memory_space_constraint(a, pltpu.HBM) for a in operands])
+    return pl.pallas_call(
+        write_out,
+        out_shape=(
+            pltpu.HBM(base_flow.shape, F32),
+            pltpu.HBM(field, F32),
+        ),
+        in_specs=[pl.BlockSpec(memory_space=pl.ANY)] * 2,
+        out_specs=tuple([pl.BlockSpec(memory_space=pl.ANY)] * 2),
+        scratch_shapes=[pltpu.SemaphoreType.DMA((4,))],
+        compiler_params=pltpu.CompilerParams(vmem_limit_bytes=8 * 1024 * 1024),
+    )(*[pltpu.with_memory_space_constraint(a, pltpu.VMEM) for a in (result, pressure)])
 
 
 def solution(mesh):

time: 44.6 us -> 42.1 us (0.944)
  local copies, waits for them, and re-layouts: 2.81 us -> 0 us
    unnamed x4 -> x0, local copies, waits for them, and re-layouts: 2.81 us -> none
    pallas_call x1 -> x2, Pallas kernels: 41.1 us -> 41.4 us  [the longest x1 40.4 us: on_device(): pl.pallas_call(functools.partial(kernel, n_stream, n_vert), out_shape=(pl...]
where the time goes in v3:
time: 42.1 us; the launch traced here: 42 us
  Pallas kernels  41.4 us (98%)
  between operations  0.64 us (2%)
    pallas_call x1, Pallas kernels, on_device(): pl.pallas_call(functools.partial(kernel, n_stream, n_vert), out_shape=(pl...  40.4 us
    pallas_call x1, Pallas kernels, on_device(): pl.pallas_call(write_out, out_shape=(pltpu.HBM(base_flow.shape, F32), plt...  1 us

profile of v3, /device:TPU:1, one launch (start us, length us, event | category | flops | bytes accessed | tf_op | source)
XLA Modules:
  0.0 42.0 jit_solution(8240787417308781867)
XLA Ops:
  0.6 40.4 %shard_map.122 = (f32[3,16,16,256]{3,2,1,0:T(8,128)S(1)}, f32[16,16,256]{2,1,0:T(8,128)S(1)}) custom-call(f32[3,16,16,256]{3,2,1,0:T(8,128)} %base_h.1, f32[3,16,16,256]{3,2,1,0:T(8,128)} %adj_h.1, f32[16,16,256]{2,1,0:T(8,128)} %reac_h.1, bf16[2,512,256]{2,1,0:T(8,128)(2,1)} %constant.16.clone.kxy_h, bf16[2,256,256]{2,1,0:T(8,128)(2,1)} %constant.17.clone.kz_h, ...), custom_call_target="tpu_custom_call" | custom-call | tf_op jit(solution)/shard_map/pallas_call | solution.py:441
  41.0 1.0 %shard_map.123 = (f32[3,16,16,256]{3,2,1,0:T(8,128)}, f32[16,16,256]{2,1,0:T(8,128)}) custom-call(f32[3,16,16,256]{3,2,1,0:T(8,128)S(1)} %get-tuple-element.4.result, f32[16,16,256]{2,1,0:T(8,128)S(1)} %get-tuple-element.5.pressure), custom_call_target="tpu_custom_call" | custom-call | tf_op jit(solution)/shard_map/pallas_call | solution.py:454

commit v4 on v3

--- a/solution.py
+++ b/solution.py
@@ -14,7 +14,8 @@
 F32 = jnp.float32
 BF16 = jnp.bfloat16
 SIDES = ((1, 0), (-1, 0), (0, 1), (0, -1), (1, 1), (1, -1), (-1, 1), (-1, -1))
-FIELDS = (3, 1, 1, 4, 6)
+FIELDS = (3, 1, 1, 1, 6, 3)
+X_UP, X_DOWN, Y_UP, Y_DOWN, CORNERS, POINTS, STRIPS = 0, 16, 32, 48, 64, 80, 256
 
 
 def gll_tables():
@@ -74,6 +75,11 @@
         * np.tile(twice, ny // 8)[None, :, None]
         * np.tile(twice, nz // 8)[None, None, :]
     )
+    ghost_rhs = ghost_matrices(turned)
+    ghost_weights = np.zeros((POINTS, nz), np.float32)
+    for top, face in ((X_UP, weights[0]), (X_DOWN, weights[-1]), (Y_UP, weights[:, 0]), (Y_DOWN, weights[:, -1])):
+        ghost_weights[top:top + 16] = face
+    ghost_weights[CORNERS:CORNERS + 4] = weights[0, 0]
     return [
         halves(np.concatenate([along_x(table), along_y(table)], axis=0)),
         halves(along_z(table)),
@@ -83,7 +89,47 @@
         halves(along_z(stiff)),
         weights,
         (1.0 / mult).astype(np.float32),
+        halves(np.concatenate([ghost_rhs[0], ghost_rhs[1]], axis=1)),
+        halves(ghost_matrices(stiff).sum(axis=0)),
+        ghost_weights,
+        (time_step / (mult * weights)[:8, 0]).astype(np.float32),
     ]
+
+
+def corner_row(sx, sy):
+    return CORNERS + (0 if sx > 0 else 2) + (0 if sy > 0 else 1)
+
+
+def strip_row(kind, sx, sy):
+    if kind == "x":
+        return POINTS + (0 if sx > 0 else 16) + (8 if sy > 0 else 0)
+    if kind == "y":
+        return POINTS + 32 + (0 if sy > 0 else 16) + (8 if sx > 0 else 0)
+    return POINTS + 64 + 16 * (corner_row(sx, sy) - CORNERS) + (0 if kind == "cx" else 8)
+
+
+def ghost_matrices(m):
+    along = np.zeros((2, POINTS, STRIPS))
+    blocks = np.kron(np.eye(2), m)
+    for sign in (1, -1):
+        node = 0 if sign > 0 else 7
+        others = [j for j in range(8) if j != node]
+        top_x, top_y = (X_UP, Y_UP) if sign > 0 else (X_DOWN, Y_DOWN)
+        for r in range(16):
+            along[0, top_x + r, top_x + r] += m[node, node]
+            along[1, top_x + r, top_x:top_x + 16] += blocks[r]
+            along[1, top_y + r, top_y + r] += m[node, node]
+            along[0, top_y + r, top_y:top_y + 16] += blocks[r]
+        for side in (1, -1):
+            r = 15 if side > 0 else 0
+            for j in others:
+                along[0, top_x + r, strip_row("x", sign, side) + j] += m[node, j]
+                along[1, top_y + r, strip_row("y", side, sign) + j] += m[node, j]
+                along[0, corner_row(sign, side), strip_row("cx", sign, side) + j] += m[node, j]
+                along[1, corner_row(side, sign), strip_row("cy", side, sign) + j] += m[node, j]
+            along[0, corner_row(sign, side), corner_row(sign, side)] += m[node, node]
+            along[1, corner_row(side, sign), corner_row(side, sign)] += m[node, node]
+    return along
 
 
 def split(value):
@@ -110,11 +156,12 @@
     n_stream,
     n_vert,
     base_h, adj_h, reac_h, kxy_h, kz_h, cxy_h, cz_h, bxy_h, bz_h, w_h, im_h,
+    gc_h, gb_h, gw_h, sc_h,
     out_h, pres_h,
-    base, adj, reac, kxy, kz, cxy, cz, bxy, bz, wts, imult,
+    base, adj, reac, kxy, kz, cxy, cz, bxy, bz, wts, imult, gc, gb, gw, sc,
     imass, conv, moved, loc, vec, grads, part3, outbuf, pbuf,
-    tiles, red_a, red_b,
-    in_sem, out_sem, send_sem, recv_sem, red_send, red_recv,
+    own, strips, ghost_reac, extra, tiles, red_a, red_b,
+    in_sem, out_sem, send_sem, recv_sem, strip_send, strip_recv, red_send, red_recv,
     *halo,
 ):
     me_s = lax.axis_index("stream")
@@ -124,7 +171,8 @@
 
     inputs = [
         (kxy_h, kxy), (kz_h, kz), (adj_h, adj), (base_h, base), (w_h, wts), (im_h, imult),
-        (cxy_h, cxy), (cz_h, cz), (bxy_h, bxy), (bz_h, bz), (reac_h, reac),
+        (cxy_h, cxy), (cz_h, cz), (reac_h, reac), (gc_h, gc), (sc_h, sc), (gw_h, gw),
+        (bxy_h, bxy), (bz_h, bz), (gb_h, gb),
     ]
     loads = [pltpu.make_async_copy(a, b, in_sem.at[i]) for i, (a, b) in enumerate(inputs)]
     for load in loads:
@@ -132,6 +180,9 @@
 
     def near(ds, dv):
         return (lax.rem(me_s + ds + n_stream, n_stream), lax.rem(me_v + dv + n_vert, n_vert))
+
+    strips[...] = jnp.zeros_like(strips)
+    ghost_reac[...] = jnp.zeros_like(ghost_reac)
 
     barrier = pltpu.get_barrier_semaphore()
     partners = [near(ds, dv) for ds, dv in SIDES]
@@ -197,27 +248,136 @@
             )
         for copy, (ds, dv) in zip(made, SIDES):
             pl.when(exists(ds, dv))(copy.start)
+        return [[copy] for copy in made]
+
+    def strip_copies(pair, field_x, field_y, along_x, along_y):
+        made = []
+        count = 0
+        for ds, dv in SIDES:
+            mine = []
+            here_x, here_y = (nx - 1 if ds > 0 else 0), (ny - 1 if dv > 0 else 0)
+            part_x, part_y = pl.ds(nx - 8 if ds > 0 else 0, 8), pl.ds(ny - 8 if dv > 0 else 0, 8)
+            if dv == 0:
+                for sy in (1, -1):
+                    mine.append((field_x.at[part_x, ny - 1 if sy > 0 else 0, :], along_x, strip_row("cx", -ds, sy)))
+            elif ds == 0:
+                for sx in (1, -1):
+                    mine.append((field_y.at[nx - 1 if sx > 0 else 0, part_y, :], along_y, strip_row("cy", sx, -dv)))
+            else:
+                mine.append((field_x.at[part_x, here_y, :], along_x, strip_row("x", -ds, -dv)))
+                mine.append((field_y.at[here_x, part_y, :], along_y, strip_row("y", -ds, -dv)))
+            group = []
+            for src, which, at in mine:
+                group.append(
+                    pltpu.make_async_remote_copy(
+                        src_ref=src, dst_ref=strips.at[which, pl.ds(at, 8), :],
+                        send_sem=strip_send.at[pair, count], recv_sem=strip_recv.at[pair, count],
+                        device_id=near(ds, dv), device_id_type=MESH,
+                    )
+                )
+                count += 1
+            made.append(group)
+        return launch(made)
+
+    def reaction_copies():
+        made = []
+        for n, (ds, dv) in enumerate(SIDES):
+            here_x, here_y = (nx - 1 if ds > 0 else 0), (ny - 1 if dv > 0 else 0)
+            if dv == 0:
+                src, at, size = reac.at[here_x], (X_UP if ds < 0 else X_DOWN), 16
+            elif ds == 0:
+                src, at, size = reac.at[:, here_y, :], (Y_UP if dv < 0 else Y_DOWN), 16
+            else:
+                src, at, size = reac.at[here_x, pl.ds(here_y, 1), :], corner_row(-ds, -dv), 1
+            made.append([
+                pltpu.make_async_remote_copy(
+                    src_ref=src, dst_ref=ghost_reac.at[pl.ds(at, size), :],
+                    send_sem=send_sem.at[6, n], recv_sem=recv_sem.at[6, n],
+                    device_id=near(ds, dv), device_id_type=MESH,
+                )
+            ])
+        return launch(made)
+
+    def launch(made):
+        for group, (ds, dv) in zip(made, SIDES):
+            @pl.when(exists(ds, dv))
+            def _(group=group):
+                for copy in group:
+                    copy.start()
         return made
 
     def arrive(made):
-        for copy, (ds, dv) in zip(made, SIDES):
-            pl.when(exists(-ds, -dv))(copy.wait_recv)
+        for group, (ds, dv) in zip(made, SIDES):
+            @pl.when(exists(-ds, -dv))
+            def _(group=group):
+                for copy in group:
+                    copy.wait_recv()
 
     def leave(made):
-        for copy, (ds, dv) in zip(made, SIDES):
-            pl.when(exists(ds, dv))(copy.wait_send)
-
-    def with_halo(e, f, src, i):
+        for group, (ds, dv) in zip(made, SIDES):
+            @pl.when(exists(ds, dv))
+            def _(group=group):
+                for copy in group:
+                    copy.wait_send()
+
+    def with_halo(e, f, src, i, more=False):
         xs, ys, cs = halo[3 * e:3 * e + 3]
-        low = src[f, i, 0:8, :] + jnp.where((sub == 0) & has_yl, ys[0, f, i], 0.0)
-        high = src[f, i, ny - 8:ny, :] + jnp.where((sub == 7) & has_yh, ys[1, f, i], 0.0)
+        low, high = ys[0, f, i], ys[1, f, i]
+        if more:
+            low = low + extra[Y_DOWN + i:Y_DOWN + i + 1]
+            high = high + extra[Y_UP + i:Y_UP + i + 1]
+        low = src[f, i, 0:8, :] + jnp.where((sub == 0) & has_yl, low, 0.0)
+        high = src[f, i, ny - 8:ny, :] + jnp.where((sub == 7) & has_yh, high, 0.0)
         value = jnp.concatenate([low, high], axis=0)
         if i in (0, nx - 1):
             side = 0 if i == 0 else 1
+            sx = -1 if i == 0 else 1
             there = has_xl if i == 0 else has_xh
             known = ((row == 0) & has_yl) | ((row == ny - 1) & has_yh)
-            value = value + jnp.where(there, xs[side, f] + jnp.where(known, cs[side, f], 0.0), 0.0)
+            face, corner = xs[side, f], cs[side, f]
+            if more:
+                top = X_UP if sx > 0 else X_DOWN
+                face = face + extra[top:top + 16]
+                below, above = corner_row(sx, -1), corner_row(sx, 1)
+                corner = corner + jnp.where(row == 0, extra[below:below + 1], extra[above:above + 1])
+            value = value + jnp.where(there, face + jnp.where(known, corner, 0.0), 0.0)
         return value
+
+    def ghost_points(e, f, value, i, which, scale=None):
+        xs, ys, cs = halo[3 * e:3 * e + 3]
+
+        def put(at, size, mine, theirs, weight, there):
+            rest = mine - theirs
+            if scale is not None:
+                rest = rest * weight
+            strips[which, at:at + size, :] = jnp.where(there, rest, 0.0)
+
+        by = [None] * 3 if scale is None else [scale, scale[0:1], scale[ny - 1:ny]]
+        put(Y_DOWN + i, 1, value[0:1], ys[0, f, i, 0:1, :], by[1], has_yl)
+        put(Y_UP + i, 1, value[ny - 1:ny], ys[1, f, i, 7:8, :], by[2], has_yh)
+        if i in (0, nx - 1):
+            side = 0 if i == 0 else 1
+            sx = -1 if i == 0 else 1
+            there = has_xl if i == 0 else has_xh
+            put(X_UP if sx > 0 else X_DOWN, 16, value, xs[side, f], by[0], there)
+            put(corner_row(sx, -1), 1, value[0:1], cs[side, f, 0:1, :], by[1], there & has_yl)
+            put(corner_row(sx, 1), 1, value[ny - 1:ny], cs[side, f, ny - 1:ny, :], by[2], there & has_yh)
+
+    lane_p = lax.broadcasted_iota(jnp.int32, (POINTS, nz), 1) % 8
+    row_p = lax.broadcasted_iota(jnp.int32, (POINTS, nz), 0)
+
+    def fold_points(value):
+        up = pltpu.roll(value, nz - 1, 1)
+        down = pltpu.roll(value, 1, 1)
+        value = value + jnp.where(lane_p == 7, up, 0.0) + jnp.where(lane_p == 0, down, 0.0)
+        up = pltpu.roll(value, POINTS - 1, 0)
+        down = pltpu.roll(value, 1, 0)
+        on_face = row_p < CORNERS
+        extra[...] = (
+            value
+            + jnp.where(on_face & (row_p % 16 == 7), up, 0.0)
+            + jnp.where(on_face & (row_p % 16 == 8), down, 0.0)
+        )
 
     def operate(value, parts):
         return wts[...].reshape(rows, nz) * (
@@ -253,11 +413,6 @@
         conv[1] -= (a * both[rows:]).reshape(nx, ny, nz)
         conv[2] -= (a * right(parts, kz)).reshape(nx, ny, nz)
     loads[4].wait()
-    for c in range(3):
-        fold_store(flat(conv.at[c]) * flat(wts), part3.at[c])
-    pl.semaphore_wait(barrier, len(partners))
-    sends = [copies(0, part3)]
-
     loads[5].wait()
     for i in range(nx):
         value = imult[i]
@@ -266,46 +421,75 @@
         if i in (0, nx - 1):
             value = value * jnp.where((me_s == 0) if i == 0 else (me_s == n_stream - 1), 2.0, 1.0)
         imult[i] = value
-        imass[i] = value / wts[i]
-    for i in range(6, 11):
+        imass[i] = time_step * value / wts[i]
+    for c in range(3):
+        fold_store(flat(conv.at[c]) * flat(wts), part3.at[c])
+    pl.semaphore_wait(barrier, len(partners))
+    sends = [copies(0, part3), strip_copies(0, part3.at[0], part3.at[1], 0, 1)]
+
+    def right_side(fields):
+        pair = jnp.concatenate([fields[0], fields[1]], axis=0)
+        return flat(wts) * (left(cxy, split(pair)) + right(split(fields[2]), cz))
+
+    for i in range(6, len(loads)):
         loads[i].wait()
+    fold_store(
+        right_side([flat(adj.at[c]) + flat(imass) * flat(part3.at[c]) for c in range(3)]),
+        loc.at[0].at[0],
+    )
+    sends += [copies(1, loc.at[0]), reaction_copies()]
 
     arrive(sends[0])
     for c in range(3):
         for i in range(nx):
-            moved[c, i] = adj[c, i] + time_step * with_halo(0, c, part3, i) * imass[i]
-
-    pair = jnp.concatenate([flat(moved.at[0]), flat(moved.at[1])], axis=0)
-    rhs = left(cxy, split(pair)) + right(split(flat(moved.at[2])), cz)
-    fold_store(rhs * flat(wts), loc.at[0].at[0])
-    sends.append(copies(1, loc.at[0]))
+            value = with_halo(0, c, part3, i)
+            moved[c, i] = adj[c, i] + value * imass[i]
+            ghost_points(0, c, value, i, c, imass[i])
+    fold_store(right_side([flat(moved.at[c]) for c in range(3)]), own.at[0])
     arrive(sends[1])
+    for c in (0, 1):
+        for at in range(POINTS, 208, 8):
+            strips[c, at:at + 8, :] = strips[c, at:at + 8, :] * sc[...]
+    ghosts = jnp.concatenate([strips[0], strips[1]], axis=0)
+    fold_points(gw[...] * (left(gc, split(ghosts)) + right(split(strips[2, 0:POINTS, :]), cz)))
+    arrive(sends[2])
     for i in range(nx):
-        vec[0, i] = with_halo(1, 0, loc.at[0], i)
+        vec[0, i] = with_halo(1, 0, own, i, True)
 
     v = flat(vec.at[0])
     parts = split(v)
     image = operate(v, parts)
     fold_store(image, loc.at[1].at[0])
-    sends.append(copies(2, loc.at[1]))
+    sends += [copies(2, loc.at[1]), strip_copies(1, loc.at[1].at[0], loc.at[1].at[0], 3, 3)]
+    first = flat(loc.at[1].at[0])
+    fold_store(operate(first, split(first)), loc.at[2].at[0])
+    sends.append(copies(3, loc.at[2]))
     to_row(v * v * flat(imult), 0)
     to_row(v * image, 1)
-    gradient(parts, 0, grads, 1)
-    arrive(sends[2])
+    gradient(parts, 0, grads, 0)
+    sends.append(copies(5, grads))
+    arrive(sends[3])
+    arrive(sends[4])
     for i in range(nx):
-        vec[1, i] = with_halo(2, 0, loc.at[1], i)
+        value = with_halo(2, 0, loc.at[1], i)
+        vec[1, i] = value
+        ghost_points(2, 0, value, i, 3)
 
     v = flat(vec.at[1])
     parts = split(v)
     image = operate(v, parts)
-    fold_store(image, grads.at[0])
-    sends.append(copies(3, grads))
+    fold_store(image, own.at[0])
+    arrive(sends[5])
+    points = strips[3, 0:POINTS, :]
+    fold_points(
+        gw[...] * (left(gb, split(strips[3])) + right(split(points), bz) + ghost_reac[...] * points)
+    )
     to_row(v * v * flat(imult), 2)
     to_row(v * image, 3)
+    arrive(sends[6])
+    for i in range(nx):
+        vec[2, i] = with_halo(3, 0, own, i, True)
     gradient(parts, 1, outbuf, 0)
-    arrive(sends[3])
-    for i in range(nx):
-        vec[2, i] = with_halo(3, 0, grads, i)
 
     v = flat(vec.at[2])
     parts = split(v)
@@ -343,10 +527,11 @@
     red_b[n_stream - 1:n_stream, :] = jnp.sum(red_a[...], axis=0, keepdims=True)
     spread(red_b, n_stream, 1)
 
+    arrive(sends[7])
     for d in range(3):
         for i in range(nx):
-            conv[d, i] = with_halo(3, 1 + d, grads, i) * imass[i]
-    arrive(sends[4])
+            conv[d, i] = with_halo(5, d, grads, i) * imass[i]
+    arrive(sends[8])
     for d in range(3):
         for i in range(nx):
             base[d, i] = with_halo(4, d, outbuf, i) * imass[i]
@@ -375,6 +560,7 @@
     c0 = a0 + a1 * k1 + a2 * f0
     c1 = a2 * f1 - a1 * a0
     c2 = a2 * f2
+    d0, d1, d2 = [c * (1.0 / time_step) for c in (c0, c1, c2)]
 
     outs = []
     for i in range(nx):
@@ -383,7 +569,7 @@
     outs[-1].start()
     for d in range(3):
         for i in range(nx):
-            moved[d, i] = moved[d, i] - (c0 * conv[d, i] + c1 * base[d, i] + c2 * adj[d, i])
+            moved[d, i] = moved[d, i] - (d0 * conv[d, i] + d1 * base[d, i] + d2 * adj[d, i])
         outs.append(pltpu.make_async_copy(moved.at[d], out_h.at[d], out_sem.at[d]))
         outs[-1].start()
     for made in sends:
@@ -416,19 +602,25 @@
         pltpu.VMEM(field, F32),
         pltpu.VMEM((3, *field), F32),
         pltpu.VMEM((3, *field), F32),
-        pltpu.VMEM((2, 1, *field), F32),
+        pltpu.VMEM((3, 1, *field), F32),
         pltpu.VMEM((3, *field), F32),
-        pltpu.VMEM((4, *field), F32),
+        pltpu.VMEM((3, *field), F32),
         pltpu.VMEM((3, *field), F32),
         pltpu.VMEM((6, *field), F32),
         pltpu.VMEM(field, F32),
+        pltpu.VMEM((1, *field), F32),
+        pltpu.VMEM((4, STRIPS, nz), F32),
+        pltpu.VMEM((POINTS, nz), F32),
+        pltpu.VMEM((POINTS, nz), F32),
         pltpu.VMEM((8, 128), F32),
         pltpu.VMEM((n_vert, 128), F32),
         pltpu.VMEM((n_stream, 128), F32),
-        pltpu.SemaphoreType.DMA((11,)),
+        pltpu.SemaphoreType.DMA((3 + len(consts),)),
         pltpu.SemaphoreType.DMA((4,)),
-        pltpu.SemaphoreType.DMA((5, 8)),
-        pltpu.SemaphoreType.DMA((5, 8)),
+        pltpu.SemaphoreType.DMA((7, 8)),
+        pltpu.SemaphoreType.DMA((7, 8)),
+        pltpu.SemaphoreType.DMA((2, 16)),
+        pltpu.SemaphoreType.DMA((2, 16)),
         pltpu.SemaphoreType.DMA((2,)),
         pltpu.SemaphoreType.DMA((2,)),
     ]
@@ -444,7 +636,7 @@
             pltpu.VMEM(base_flow.shape, F32),
             pltpu.VMEM(field, F32),
         ),
-        in_specs=[pl.BlockSpec(memory_space=pl.ANY)] * 11,
+        in_specs=[pl.BlockSpec(memory_space=pl.ANY)] * len(operands),
         out_specs=(pl.BlockSpec(memory_space=pl.ANY), pl.BlockSpec(memory_space=pl.ANY)),
         scratch_shapes=scratch,
         compiler_params=pltpu.CompilerParams(

time: 42.1 us -> 37 us (0.88)
  Pallas kernels: 41.4 us -> 36.3 us
    pallas_call x1, Pallas kernels: 40.4 us -> 35.3 us  [on_device(): pl.pallas_call(functools.partial(kernel, n_stream, n_vert), out_shape=(pl...]
where the time goes in v4:
time: 37 us
  Pallas kernels  36.3 us (98%)
  between operations  0.64 us (2%)
    pallas_call x1, Pallas kernels, on_device(): pl.pallas_call(functools.partial(kernel, n_stream, n_vert), out_shape=(pl...  35.3 us
    pallas_call x1, Pallas kernels, on_device(): pl.pallas_call(write_out, out_shape=(pltpu.HBM(base_flow.shape, F32), plt...  1 us

profile of v4, /device:TPU:1, one launch (start us, length us, event | category | flops | bytes accessed | tf_op | source)
XLA Modules:
  0.0 37.0 jit_solution(10439332641322373742)
XLA Ops:
  0.6 35.3 %shard_map.158 = (f32[3,16,16,256]{3,2,1,0:T(8,128)S(1)}, f32[16,16,256]{2,1,0:T(8,128)S(1)}) custom-call(f32[3,16,16,256]{3,2,1,0:T(8,128)} %base_h.1, f32[3,16,16,256]{3,2,1,0:T(8,128)} %adj_h.1, f32[16,16,256]{2,1,0:T(8,128)} %reac_h.1, bf16[2,512,256]{2,1,0:T(8,128)(2,1)} %constant.24.clone.kxy_h, bf16[2,256,256]{2,1,0:T(8,128)(2,1)} %constant.25.clone.kz_h, ...), custom_call_target="tpu_custom_call" | custom-call | tf_op jit(solution)/shard_map/pallas_call | solution.py:633
  36.0 1.0 %shard_map.159 = (f32[3,16,16,256]{3,2,1,0:T(8,128)}, f32[16,16,256]{2,1,0:T(8,128)}) custom-call(f32[3,16,16,256]{3,2,1,0:T(8,128)S(1)} %get-tuple-element.4.result, f32[16,16,256]{2,1,0:T(8,128)S(1)} %get-tuple-element.5.pressure), custom_call_target="tpu_custom_call" | custom-call | tf_op jit(solution)/shard_map/pallas_call | solution.py:646

commit v5 on v4

--- a/solution.py
+++ b/solution.py
@@ -14,7 +14,7 @@
 F32 = jnp.float32
 BF16 = jnp.bfloat16
 SIDES = ((1, 0), (-1, 0), (0, 1), (0, -1), (1, 1), (1, -1), (-1, 1), (-1, -1))
-FIELDS = (3, 1, 1, 1, 6, 3)
+FIELDS = (3, 1, 1, 1, 2, 1)
 X_UP, X_DOWN, Y_UP, Y_DOWN, CORNERS, POINTS, STRIPS = 0, 16, 32, 48, 64, 80, 256
 
 
@@ -80,15 +80,18 @@
     for top, face in ((X_UP, weights[0]), (X_DOWN, weights[-1]), (Y_UP, weights[:, 0]), (Y_DOWN, weights[:, -1])):
         ghost_weights[top:top + 16] = face
     ghost_weights[CORNERS:CORNERS + 4] = weights[0, 0]
+    first = np.zeros((nx, nz))
+    for r in range(nx):
+        first[r] = np.tile(np.repeat(table[r % 8], ny), nx // 8) * (np.arange(nz) // 128 == r // 8)
+    across = np.tile(quad[:, None] * quad[None, :], (1, nz // 8))
     return [
-        halves(np.concatenate([along_x(table), along_y(table)], axis=0)),
-        halves(along_z(table)),
+        np.concatenate(
+            [np.tile(table.T, (1, nz // 8)), np.tile(table, (1, nz // 8)), first, across, 1.0 / mult[1, :8]]
+        ).astype(np.float32),
         halves(np.concatenate([along_x(turned), along_y(turned)], axis=1)),
         halves(along_z(turned)),
         halves(along_x(stiff) + along_y(stiff)),
         halves(along_z(stiff)),
-        weights,
-        (1.0 / mult).astype(np.float32),
         halves(np.concatenate([ghost_rhs[0], ghost_rhs[1]], axis=1)),
         halves(ghost_matrices(stiff).sum(axis=0)),
         ghost_weights,
@@ -155,13 +158,13 @@
 def kernel(
     n_stream,
     n_vert,
-    base_h, adj_h, reac_h, kxy_h, kz_h, cxy_h, cz_h, bxy_h, bz_h, w_h, im_h,
+    base_h, adj_h, reac_h, tab_h, cxy_h, cz_h, bxy_h, bz_h,
     gc_h, gb_h, gw_h, sc_h,
-    out_h, pres_h,
-    base, adj, reac, kxy, kz, cxy, cz, bxy, bz, wts, imult, gc, gb, gw, sc,
-    imass, conv, moved, loc, vec, grads, part3, outbuf, pbuf,
+    moved, asm, vec, coef,
+    base, adj, reac, tab, cxy, cz, bxy, bz, gc, gb, gw, sc, kxy, kz, wts, imult,
+    imass, conv, loc, raw, part3,
     own, strips, ghost_reac, extra, tiles, red_a, red_b,
-    in_sem, out_sem, send_sem, recv_sem, strip_send, strip_recv, red_send, red_recv,
+    in_sem, send_sem, recv_sem, strip_send, strip_recv, red_send, red_recv,
     *halo,
 ):
     me_s = lax.axis_index("stream")
@@ -170,12 +173,12 @@
     rows = nx * ny
 
     inputs = [
-        (kxy_h, kxy), (kz_h, kz), (adj_h, adj), (base_h, base), (w_h, wts), (im_h, imult),
+        (tab_h, tab), (adj_h, adj), (base_h, base),
         (cxy_h, cxy), (cz_h, cz), (reac_h, reac), (gc_h, gc), (sc_h, sc), (gw_h, gw),
         (bxy_h, bxy), (bz_h, bz), (gb_h, gb),
     ]
     loads = [pltpu.make_async_copy(a, b, in_sem.at[i]) for i, (a, b) in enumerate(inputs)]
-    for load in loads:
+    for load in loads[:3]:
         load.start()
 
     def near(ds, dv):
@@ -300,7 +303,7 @@
 
     def launch(made):
         for group, (ds, dv) in zip(made, SIDES):
-            @pl.when(exists(ds, dv))
+            @pl.when(bool(group) and exists(ds, dv))
             def _(group=group):
                 for copy in group:
                     copy.start()
@@ -308,14 +311,14 @@
 
     def arrive(made):
         for group, (ds, dv) in zip(made, SIDES):
-            @pl.when(exists(-ds, -dv))
+            @pl.when(bool(group) and exists(-ds, -dv))
             def _(group=group):
                 for copy in group:
                     copy.wait_recv()
 
     def leave(made):
         for group, (ds, dv) in zip(made, SIDES):
-            @pl.when(exists(ds, dv))
+            @pl.when(bool(group) and exists(ds, dv))
             def _(group=group):
                 for copy in group:
                     copy.wait_send()
@@ -384,26 +387,103 @@
             left(bxy, parts) + right(parts, bz) + flat(reac) * value
         )
 
-    def gradient(parts, k, dst, at):
-        w = wts[...].reshape(rows, nz)
+    def slopes(parts, k):
         both = left(kxy, parts)
-        fold_store(w * both[:rows], dst.at[at])
-        fold_store(w * both[rows:], dst.at[at + 1])
-        fold_store(w * right(parts, kz), dst.at[at + 2])
+        raw[k, 0] = both[:rows].reshape(nx, ny, nz)
+        raw[k, 1] = both[rows:].reshape(nx, ny, nz)
+        third = right(parts, kz)
+        for i in range(nx):
+            v = third[i * ny:(i + 1) * ny]
+            other = jnp.where(lane == 7, pltpu.roll(v, nz - 1, 1), pltpu.roll(v, 1, 1))
+            asm[k, 2, i] = jnp.where((lane == 7) | (lane == 0), 0.5 * (v + other), v)
+
+    def slope_copies(e, first, count):
+        xs, ys = halo[3 * e:3 * e + 2]
+        made = []
+        for n, (ds, dv) in enumerate(SIDES):
+            group = []
+            if ds * dv == 0:
+                some = pl.ds(first, count)
+                if dv == 0:
+                    a = raw.at[some, 0, nx - 1 if ds > 0 else 0]
+                    b = xs.at[0 if ds > 0 else 1]
+                else:
+                    a = raw.at[some, 1, :, pl.ds(ny - 1 if dv > 0 else 0, 1), :]
+                    b = ys.at[0 if dv > 0 else 1].at[:, :, pl.ds(0 if dv > 0 else 7, 1), :]
+                group.append(
+                    pltpu.make_async_remote_copy(
+                        src_ref=a, dst_ref=b,
+                        send_sem=send_sem.at[e, n], recv_sem=recv_sem.at[e, n],
+                        device_id=near(ds, dv), device_id_type=MESH,
+                    )
+                )
+            made.append(group)
+        return launch(made)
+
+    def average(e, f, k):
+        xs, ys = halo[3 * e:3 * e + 2]
+        middle = 0.5 * (raw[k, 0, 7] + raw[k, 0, 8])
+        for i in range(nx):
+            v = raw[k, 0, i]
+            if i in (7, 8):
+                v = middle
+            elif i == 0:
+                v = jnp.where(has_xl, 0.5 * (v + xs[0, f]), v)
+            elif i == nx - 1:
+                v = jnp.where(has_xh, 0.5 * (v + xs[1, f]), v)
+            asm[k, 0, i] = v
+            v = raw[k, 1, i]
+            other = jnp.concatenate([ys[0, f, i], ys[1, f, i]], axis=0)
+            other = jnp.where(row == 7, pltpu.roll(v, ny - 1, 0), other)
+            other = jnp.where(row == 8, pltpu.roll(v, 1, 0), other)
+            shared = (row == 7) | (row == 8) | ((row == 0) & has_yl) | ((row == ny - 1) & has_yh)
+            asm[k, 1, i] = jnp.where(shared, 0.5 * (v + other), v)
 
     def to_row(value, slot):
         s = value.reshape(rows // 8, 8, nz).sum(axis=0)
         s = s[:, :128] + s[:, 128:]
         tiles[slot:slot + 1, :] = jnp.sum(s, axis=0, keepdims=True)
 
-    for i in range(4):
-        loads[i].wait()
+    _, quad = gll_tables()
+    loads[0].wait()
+    column = lax.broadcasted_iota(jnp.int32, (ny, nz), 1)
+
+    def put_block(dst, at, mask, tile):
+        high = tile.astype(BF16).astype(F32)
+        dst[0, at:at + ny, :] = jnp.where(mask, high, 0.0).astype(BF16)
+        dst[1, at:at + ny, :] = jnp.where(mask, tile - high, 0.0).astype(BF16)
+
+    tile_z = jnp.concatenate([tab[0:8], tab[0:8]], axis=0)
+    tile_y = jnp.concatenate([tab[8:16], tab[8:16]], axis=0)
+    tile_w = jnp.concatenate([tab[32:40], tab[32:40]], axis=0)
+    tile_m = jnp.concatenate([tab[40:48], tab[40:48]], axis=0)
+    edge = ((row == 0) & (me_v == 0)) | ((row == ny - 1) & (me_v == n_vert - 1))
+    tile_m = tile_m * jnp.where(edge, 2.0, 1.0)
+    for i in range(nx):
+        here = column // 8 == 2 * i + row // 8
+        put_block(kz, i * ny, here, tile_z)
+        put_block(kxy, rows + i * ny, here, tile_y)
+        put_block(kxy, i * ny, column % ny == row, jnp.broadcast_to(tab[16 + i:17 + i], (ny, nz)))
+        wts[i] = tile_w * float(quad[i % 8])
+        value = tile_m
+        if i in (0, nx - 1):
+            value = value * jnp.where((me_s == 0) if i == 0 else (me_s == n_stream - 1), 1.0, 0.5)
+        elif i % 8 in (0, 7):
+            value = value * 0.5
+        imult[i] = value
+        imass[i] = time_step * value / wts[i]
+
+    loads[1].wait()
     for c in range(3):
         parts = split(flat(adj.at[c]))
         both = left(kxy, parts)
+        third = right(parts, kz)
+        if c == 0:
+            loads[2].wait()
+            for load in loads[3:]:
+                load.start()
         conv[c] = (
-            flat(base.at[0]) * both[:rows] + flat(base.at[1]) * both[rows:]
-            + flat(base.at[2]) * right(parts, kz)
+            flat(base.at[0]) * both[:rows] + flat(base.at[1]) * both[rows:] + flat(base.at[2]) * third
         ).reshape(nx, ny, nz)
     for j in range(3):
         parts = split(flat(base.at[j]))
@@ -412,16 +492,6 @@
         conv[0] -= (a * both[:rows]).reshape(nx, ny, nz)
         conv[1] -= (a * both[rows:]).reshape(nx, ny, nz)
         conv[2] -= (a * right(parts, kz)).reshape(nx, ny, nz)
-    loads[4].wait()
-    loads[5].wait()
-    for i in range(nx):
-        value = imult[i]
-        edge = ((row == 0) & (me_v == 0)) | ((row == ny - 1) & (me_v == n_vert - 1))
-        value = value * jnp.where(edge, 2.0, 1.0)
-        if i in (0, nx - 1):
-            value = value * jnp.where((me_s == 0) if i == 0 else (me_s == n_stream - 1), 2.0, 1.0)
-        imult[i] = value
-        imass[i] = time_step * value / wts[i]
     for c in range(3):
         fold_store(flat(conv.at[c]) * flat(wts), part3.at[c])
     pl.semaphore_wait(barrier, len(partners))
@@ -431,8 +501,8 @@
         pair = jnp.concatenate([fields[0], fields[1]], axis=0)
         return flat(wts) * (left(cxy, split(pair)) + right(split(fields[2]), cz))
 
-    for i in range(6, len(loads)):
-        loads[i].wait()
+    for load in loads[3:]:
+        load.wait()
     fold_store(
         right_side([flat(adj.at[c]) + flat(imass) * flat(part3.at[c]) for c in range(3)]),
         loc.at[0].at[0],
@@ -466,8 +536,8 @@
     sends.append(copies(3, loc.at[2]))
     to_row(v * v * flat(imult), 0)
     to_row(v * image, 1)
-    gradient(parts, 0, grads, 0)
-    sends.append(copies(5, grads))
+    slopes(parts, 0)
+    sends.append(slope_copies(5, 0, 1))
     arrive(sends[3])
     arrive(sends[4])
     for i in range(nx):
@@ -489,7 +559,6 @@
     arrive(sends[6])
     for i in range(nx):
         vec[2, i] = with_halo(3, 0, own, i, True)
-    gradient(parts, 1, outbuf, 0)
 
     v = flat(vec.at[2])
     parts = split(v)
@@ -521,21 +590,18 @@
         )
 
     spread(red_a, n_vert, 0)
-    gradient(parts, 2, outbuf, 3)
-    sends.append(copies(4, outbuf))
+    slopes(split(flat(vec.at[1])), 1)
+    slopes(parts, 2)
+    sends.append(slope_copies(4, 1, 2))
     whole(red_a, n_vert, 0).wait_recv()
     red_b[n_stream - 1:n_stream, :] = jnp.sum(red_a[...], axis=0, keepdims=True)
     spread(red_b, n_stream, 1)
 
     arrive(sends[7])
-    for d in range(3):
-        for i in range(nx):
-            conv[d, i] = with_halo(5, d, grads, i) * imass[i]
+    average(5, 0, 0)
     arrive(sends[8])
-    for d in range(3):
-        for i in range(nx):
-            base[d, i] = with_halo(4, d, outbuf, i) * imass[i]
-            adj[d, i] = with_halo(4, 3 + d, outbuf, i) * imass[i]
+    average(4, 0, 1)
+    average(4, 1, 2)
 
     whole(red_b, n_stream, 1).wait_recv()
     total = jnp.sum(red_b[...], axis=0, keepdims=True)
@@ -560,31 +626,27 @@
     c0 = a0 + a1 * k1 + a2 * f0
     c1 = a2 * f1 - a1 * a0
     c2 = a2 * f2
-    d0, d1, d2 = [c * (1.0 / time_step) for c in (c0, c1, c2)]
-
-    outs = []
-    for i in range(nx):
-        pbuf[i] = c0 * vec[0, i] + c1 * vec[1, i] + c2 * vec[2, i]
-    outs.append(pltpu.make_async_copy(pbuf, pres_h, out_sem.at[3]))
-    outs[-1].start()
-    for d in range(3):
-        for i in range(nx):
-            moved[d, i] = moved[d, i] - (d0 * conv[d, i] + d1 * base[d, i] + d2 * adj[d, i])
-        outs.append(pltpu.make_async_copy(moved.at[d], out_h.at[d], out_sem.at[d]))
-        outs[-1].start()
+    for k, c in enumerate((c0, c1, c2)):
+        coef[k:k + 1, :] = jnp.broadcast_to(c, (1, nz))
     for made in sends:
         leave(made)
     whole(red_a, n_vert, 0).wait_send()
     whole(red_b, n_stream, 1).wait_send()
-    for copy in outs:
-        copy.wait()
-
-
-def write_out(result, pressure, out_h, pres_h, sems):
-    copies = [pltpu.make_async_copy(result.at[d], out_h.at[d], sems.at[d]) for d in range(3)]
-    copies.append(pltpu.make_async_copy(pressure, pres_h, sems.at[3]))
-    for copy in copies:
-        copy.start()
+
+
+def combine(moved, asm, vec, coef, out_h, pres_h, out, pres, sems):
+    copies = []
+    for i in range(pres.shape[0]):
+        pres[i] = coef[0:1] * vec[0, i] + coef[1:2] * vec[1, i] + coef[2:3] * vec[2, i]
+    copies.append(pltpu.make_async_copy(pres, pres_h, sems.at[3]))
+    copies[-1].start()
+    for d in range(3):
+        for i in range(pres.shape[0]):
+            out[d, i] = moved[d, i] - (
+                coef[0:1] * asm[0, d, i] + coef[1:2] * asm[1, d, i] + coef[2:3] * asm[2, d, i]
+            )
+        copies.append(pltpu.make_async_copy(out.at[d], out_h.at[d], sems.at[d]))
+        copies[-1].start()
     for copy in copies:
         copy.wait()
 
@@ -599,15 +661,15 @@
         pltpu.VMEM(base_flow.shape, F32),
         pltpu.VMEM(field, F32),
         *[pltpu.VMEM(c.shape, c.dtype) for c in consts],
+        pltpu.VMEM((2, 2 * nx * ny, nx * ny), BF16),
+        pltpu.VMEM((2, nz, nz), BF16),
+        pltpu.VMEM(field, F32),
+        pltpu.VMEM(field, F32),
         pltpu.VMEM(field, F32),
         pltpu.VMEM((3, *field), F32),
+        pltpu.VMEM((3, 1, *field), F32),
+        pltpu.VMEM((3, 2, *field), F32),
         pltpu.VMEM((3, *field), F32),
-        pltpu.VMEM((3, 1, *field), F32),
-        pltpu.VMEM((3, *field), F32),
-        pltpu.VMEM((3, *field), F32),
-        pltpu.VMEM((3, *field), F32),
-        pltpu.VMEM((6, *field), F32),
-        pltpu.VMEM(field, F32),
         pltpu.VMEM((1, *field), F32),
         pltpu.VMEM((4, STRIPS, nz), F32),
         pltpu.VMEM((POINTS, nz), F32),
@@ -616,7 +678,6 @@
         pltpu.VMEM((n_vert, 128), F32),
         pltpu.VMEM((n_stream, 128), F32),
         pltpu.SemaphoreType.DMA((3 + len(consts),)),
-        pltpu.SemaphoreType.DMA((4,)),
         pltpu.SemaphoreType.DMA((7, 8)),
         pltpu.SemaphoreType.DMA((7, 8)),
         pltpu.SemaphoreType.DMA((2, 16)),
@@ -630,30 +691,36 @@
             pltpu.VMEM((2, count, nx, 8, nz), F32),
             pltpu.VMEM((2, count, ny, nz), F32),
         ]
-    result, pressure = pl.pallas_call(
+    pieces = pl.pallas_call(
         functools.partial(kernel, n_stream, n_vert),
         out_shape=(
-            pltpu.VMEM(base_flow.shape, F32),
-            pltpu.VMEM(field, F32),
+            pltpu.VMEM((3, *field), F32),
+            pltpu.VMEM((3, 3, *field), F32),
+            pltpu.VMEM((3, *field), F32),
+            pltpu.VMEM((8, nz), F32),
         ),
         in_specs=[pl.BlockSpec(memory_space=pl.ANY)] * len(operands),
-        out_specs=(pl.BlockSpec(memory_space=pl.ANY), pl.BlockSpec(memory_space=pl.ANY)),
+        out_specs=tuple([pl.BlockSpec(memory_space=pltpu.VMEM)] * 4),
         scratch_shapes=scratch,
         compiler_params=pltpu.CompilerParams(
             collective_id=0, has_side_effects=True, vmem_limit_bytes=48 * 1024 * 1024
         ),
     )(*[pltpu.with_memory_space_constraint(a, pltpu.HBM) for a in operands])
     return pl.pallas_call(
-        write_out,
+        combine,
         out_shape=(
             pltpu.HBM(base_flow.shape, F32),
             pltpu.HBM(field, F32),
         ),
-        in_specs=[pl.BlockSpec(memory_space=pl.ANY)] * 2,
+        in_specs=[pl.BlockSpec(memory_space=pltpu.VMEM)] * 4,
         out_specs=tuple([pl.BlockSpec(memory_space=pl.ANY)] * 2),
-        scratch_shapes=[pltpu.SemaphoreType.DMA((4,))],
-        compiler_params=pltpu.CompilerParams(vmem_limit_bytes=8 * 1024 * 1024),
-    )(*[pltpu.with_memory_space_constraint(a, pltpu.VMEM) for a in (result, pressure)])
+        scratch_shapes=[
+            pltpu.VMEM(base_flow.shape, F32),
+            pltpu.VMEM(field, F32),
+            pltpu.SemaphoreType.DMA((4,)),
+        ],
+        compiler_params=pltpu.CompilerParams(vmem_limit_bytes=16 * 1024 * 1024),
+    )(*[pltpu.with_memory_space_constraint(a, pltpu.VMEM) for a in pieces])
 
 
 def solution(mesh):

time: 37 us -> 36.3 us (0.981)
  Pallas kernels: 36.3 us -> 35.5 us
    pallas_call x1, Pallas kernels: 35.3 us -> 34.5 us  [on_device(): pl.pallas_call(functools.partial(kernel, n_stream, n_vert), out_shape=(pl...]
where the time goes in v5:
time: 36.3 us; the launch traced here: 36.1 us
  Pallas kernels  35.5 us (98%)
  between operations  0.64 us (2%)
    pallas_call x1, Pallas kernels, on_device(): pl.pallas_call(functools.partial(kernel, n_stream, n_vert), out_shape=(pl...  34.5 us
    pallas_call x1, Pallas kernels, on_device(): pl.pallas_call(combine, out_shape=(pltpu.HBM(base_flow.shape, F32), pltpu...  1.04 us

profile of v5, /device:TPU:1, one launch (start us, length us, event | category | flops | bytes accessed | tf_op | source)
XLA Modules:
  0.0 36.1 jit_solution(399787893776086687)
XLA Ops:
  0.6 34.5 %shard_map.131 = (f32[3,16,16,256]{3,2,1,0:T(8,128)S(1)}, f32[3,3,16,16,256]{4,3,2,1,0:T(8,128)S(1)}, f32[3,16,16,256]{3,2,1,0:T(8,128)S(1)}, f32[8,256]{1,0:T(8,128)S(1)}) custom-call(f32[3,16,16,256]{3,2,1,0:T(8,128)} %base_h.1, f32[3,16,16,256]{3,2,1,0:T(8,128)} %adj_h.1, f32[16,16,256]{2,1,0:T(8,128)} %reac_h.1, f32[48,256]{1,0:T(8,128)} %constant.18.clone.tab_h, ...), custom_call_target="tpu_custom_call" | custom-call | tf_op jit(solution)/shard_map/pallas_call | solution.py:694
  35.1 1.0 %shard_map.132 = (f32[3,16,16,256]{3,2,1,0:T(8,128)}, f32[16,16,256]{2,1,0:T(8,128)}) custom-call(f32[3,16,16,256]{3,2,1,0:T(8,128)S(1)} %get-tuple-element.6.moved, f32[3,3,16,16,256]{4,3,2,1,0:T(8,128)S(1)} %get-tuple-element.7.asm, f32[3,16,16,256]{3,2,1,0:T(8,128)S(1)} %get-tuple-element.8.vec, f32[8,256]{1,0:T(8,128)S(1)} %get-tuple-element.9.coef), custom_call_target="tpu_custom_call" | custom-call | tf_op jit(solution)/shard_map/pallas_call | solution.py:709

commit v6 on v5

--- a/solution.py
+++ b/solution.py
@@ -15,7 +15,7 @@
 BF16 = jnp.bfloat16
 SIDES = ((1, 0), (-1, 0), (0, 1), (0, -1), (1, 1), (1, -1), (-1, 1), (-1, -1))
 FIELDS = (3, 1, 1, 1, 2, 1)
-X_UP, X_DOWN, Y_UP, Y_DOWN, CORNERS, POINTS, STRIPS = 0, 16, 32, 48, 64, 80, 256
+X_UP, X_DOWN, Y_UP, Y_DOWN, CORNERS, POINTS, STRIPS = 0, 16, 32, 48, 64, 80, 128
 
 
 def gll_tables():
@@ -76,6 +76,14 @@
         * np.tile(twice, nz // 8)[None, None, :]
     )
     ghost_rhs = ghost_matrices(turned)
+    points = np.zeros(POINTS, np.int64)
+    points[X_UP:X_UP + 16] = (nx - 1) * ny + np.arange(ny)
+    points[X_DOWN:X_DOWN + 16] = np.arange(ny)
+    points[Y_UP:Y_UP + 16] = np.arange(nx) * ny + ny - 1
+    points[Y_DOWN:Y_DOWN + 16] = np.arange(nx) * ny
+    for sx in (1, -1):
+        for sy in (1, -1):
+            points[corner_row(sx, sy)] = ((nx - 1) * ny if sx > 0 else 0) + (ny - 1 if sy > 0 else 0)
     ghost_weights = np.zeros((POINTS, nz), np.float32)
     for top, face in ((X_UP, weights[0]), (X_DOWN, weights[-1]), (Y_UP, weights[:, 0]), (Y_DOWN, weights[:, -1])):
         ghost_weights[top:top + 16] = face
@@ -94,8 +102,9 @@
         halves(along_z(stiff)),
         halves(np.concatenate([ghost_rhs[0], ghost_rhs[1]], axis=1)),
         halves(ghost_matrices(stiff).sum(axis=0)),
+        halves(np.concatenate([along_x(turned), along_y(turned)], axis=1)[points]),
+        halves((along_x(stiff) + along_y(stiff))[points]),
         ghost_weights,
-        (time_step / (mult * weights)[:8, 0]).astype(np.float32),
     ]
 
 
@@ -104,11 +113,11 @@
 
 
 def strip_row(kind, sx, sy):
-    if kind == "x":
-        return POINTS + (0 if sx > 0 else 16) + (8 if sy > 0 else 0)
-    if kind == "y":
-        return POINTS + 32 + (0 if sy > 0 else 16) + (8 if sx > 0 else 0)
-    return POINTS + 64 + 16 * (corner_row(sx, sy) - CORNERS) + (0 if kind == "cx" else 8)
+    if kind in ("x", "y"):
+        return POINTS + 2 * (corner_row(sx, sy) - CORNERS) + (kind == "y")
+    if kind == "cx":
+        return POINTS + 8 + 2 * (sx < 0) + (sy < 0)
+    return POINTS + 12 + 2 * (sy < 0) + (sx < 0)
 
 
 def ghost_matrices(m):
@@ -116,7 +125,6 @@
     blocks = np.kron(np.eye(2), m)
     for sign in (1, -1):
         node = 0 if sign > 0 else 7
-        others = [j for j in range(8) if j != node]
         top_x, top_y = (X_UP, Y_UP) if sign > 0 else (X_DOWN, Y_DOWN)
         for r in range(16):
             along[0, top_x + r, top_x + r] += m[node, node]
@@ -125,11 +133,10 @@
             along[0, top_y + r, top_y:top_y + 16] += blocks[r]
         for side in (1, -1):
             r = 15 if side > 0 else 0
-            for j in others:
-                along[0, top_x + r, strip_row("x", sign, side) + j] += m[node, j]
-                along[1, top_y + r, strip_row("y", side, sign) + j] += m[node, j]
-                along[0, corner_row(sign, side), strip_row("cx", sign, side) + j] += m[node, j]
-                along[1, corner_row(side, sign), strip_row("cy", side, sign) + j] += m[node, j]
+            along[0, top_x + r, strip_row("x", sign, side)] += 1.0
+            along[0, top_y + r, strip_row("y", side, sign)] += 1.0
+            along[0, corner_row(sign, side), strip_row("cx", sign, side)] += 1.0
+            along[0, corner_row(side, sign), strip_row("cy", side, sign)] += 1.0
             along[0, corner_row(sign, side), corner_row(sign, side)] += m[node, node]
             along[1, corner_row(side, sign), corner_row(side, sign)] += m[node, node]
     return along
@@ -159,11 +166,11 @@
     n_stream,
     n_vert,
     base_h, adj_h, reac_h, tab_h, cxy_h, cz_h, bxy_h, bz_h,
-    gc_h, gb_h, gw_h, sc_h,
+    gc_h, gb_h, cf_h, bf_h, gw_h,
     moved, asm, vec, coef,
-    base, adj, reac, tab, cxy, cz, bxy, bz, gc, gb, gw, sc, kxy, kz, wts, imult,
+    base, adj, reac, tab, cxy, cz, bxy, bz, gc, gb, cf, bf, gw, kxy, kz, wts, imult,
     imass, conv, loc, raw, part3,
-    own, strips, ghost_reac, extra, tiles, red_a, red_b,
+    own, strips, ghost_reac, extra, mine, mine_reac, outbox, inbox, strip_out, tiles, red_a, red_b,
     in_sem, send_sem, recv_sem, strip_send, strip_recv, red_send, red_recv,
     *halo,
 ):
@@ -174,8 +181,8 @@
 
     inputs = [
         (tab_h, tab), (adj_h, adj), (base_h, base),
-        (cxy_h, cxy), (cz_h, cz), (reac_h, reac), (gc_h, gc), (sc_h, sc), (gw_h, gw),
-        (bxy_h, bxy), (bz_h, bz), (gb_h, gb),
+        (cf_h, cf), (cz_h, cz), (gw_h, gw), (cxy_h, cxy), (reac_h, reac), (gc_h, gc),
+        (bxy_h, bxy), (bz_h, bz), (bf_h, bf), (gb_h, gb),
     ]
     loads = [pltpu.make_async_copy(a, b, in_sem.at[i]) for i, (a, b) in enumerate(inputs)]
     for load in loads[:3]:
@@ -186,6 +193,9 @@
 
     strips[...] = jnp.zeros_like(strips)
     ghost_reac[...] = jnp.zeros_like(ghost_reac)
+    inbox[...] = jnp.zeros_like(inbox)
+    mine[:, CORNERS + 4:, :] = jnp.zeros((3, POINTS - CORNERS - 4, nz), F32)
+    mine_reac[CORNERS + 4:, :] = jnp.zeros((POINTS - CORNERS - 4, nz), F32)
 
     barrier = pltpu.get_barrier_semaphore()
     partners = [near(ds, dv) for ds, dv in SIDES]
@@ -253,33 +263,52 @@
             pl.when(exists(ds, dv))(copy.start)
         return [[copy] for copy in made]
 
-    def strip_copies(pair, field_x, field_y, along_x, along_y):
+    def strip_copies(pair, field_x, field_y, scale, m, which):
+        def slope(node):
+            return [0.0 if j == node else float(m[node, j]) for j in range(8)]
+
+        columns = {}
+        for node in (0, 7):
+            factors = jnp.zeros((8, nz), F32)
+            for j, c in enumerate(slope(node)):
+                factors = jnp.where(sub == j, c, factors)
+            columns[node] = factors
+
+        def part(field, x, ys):
+            value = field[x, ys, :]
+            return value * imass[x, ys, :] if scale else value
+
+        def sum_x(sx, start, y):
+            terms = [c * part(field_x, start + j, slice(y, y + 1)) for j, c in enumerate(slope(0 if sx > 0 else 7)) if c]
+            return functools.reduce(jnp.add, terms)
+
+        def sum_y(sy, x, start):
+            tile = columns[0 if sy > 0 else 7] * part(field_y, x, slice(start, start + 8))
+            return jnp.sum(tile, axis=0, keepdims=True)
+
         made = []
-        count = 0
-        for ds, dv in SIDES:
-            mine = []
+        for n, (ds, dv) in enumerate(SIDES):
             here_x, here_y = (nx - 1 if ds > 0 else 0), (ny - 1 if dv > 0 else 0)
-            part_x, part_y = pl.ds(nx - 8 if ds > 0 else 0, 8), pl.ds(ny - 8 if dv > 0 else 0, 8)
+            start_x, start_y = (nx - 8 if ds > 0 else 0), (ny - 8 if dv > 0 else 0)
             if dv == 0:
-                for sy in (1, -1):
-                    mine.append((field_x.at[part_x, ny - 1 if sy > 0 else 0, :], along_x, strip_row("cx", -ds, sy)))
+                first = strip_row("cx", -ds, 1)
+                two = [sum_x(-ds, start_x, ny - 1), sum_x(-ds, start_x, 0)]
             elif ds == 0:
-                for sx in (1, -1):
-                    mine.append((field_y.at[nx - 1 if sx > 0 else 0, part_y, :], along_y, strip_row("cy", sx, -dv)))
+                first = strip_row("cy", 1, -dv)
+                two = [sum_y(-dv, nx - 1, start_y), sum_y(-dv, 0, start_y)]
             else:
-                mine.append((field_x.at[part_x, here_y, :], along_x, strip_row("x", -ds, -dv)))
-                mine.append((field_y.at[here_x, part_y, :], along_y, strip_row("y", -ds, -dv)))
-            group = []
-            for src, which, at in mine:
-                group.append(
-                    pltpu.make_async_remote_copy(
-                        src_ref=src, dst_ref=strips.at[which, pl.ds(at, 8), :],
-                        send_sem=strip_send.at[pair, count], recv_sem=strip_recv.at[pair, count],
-                        device_id=near(ds, dv), device_id_type=MESH,
-                    )
+                first = strip_row("x", -ds, -dv)
+                two = [sum_x(-ds, start_x, here_y), sum_y(-dv, here_x, start_y)]
+            at = first - POINTS
+            for k in (0, 1):
+                strip_out[pair, at + k:at + k + 1, :] = two[k]
+            made.append([
+                pltpu.make_async_remote_copy(
+                    src_ref=strip_out.at[pair, pl.ds(at, 2), :], dst_ref=strips.at[which, pl.ds(first, 2), :],
+                    send_sem=strip_send.at[pair, n], recv_sem=strip_recv.at[pair, n],
+                    device_id=near(ds, dv), device_id_type=MESH,
                 )
-                count += 1
-            made.append(group)
+            ])
         return launch(made)
 
     def reaction_copies():
@@ -325,10 +354,10 @@
 
     def with_halo(e, f, src, i, more=False):
         xs, ys, cs = halo[3 * e:3 * e + 3]
-        low, high = ys[0, f, i], ys[1, f, i]
         if more:
-            low = low + extra[Y_DOWN + i:Y_DOWN + i + 1]
-            high = high + extra[Y_UP + i:Y_UP + i + 1]
+            low, high = extra[Y_DOWN + i:Y_DOWN + i + 1], extra[Y_UP + i:Y_UP + i + 1]
+        else:
+            low, high = ys[0, f, i], ys[1, f, i]
         low = src[f, i, 0:8, :] + jnp.where((sub == 0) & has_yl, low, 0.0)
         high = src[f, i, ny - 8:ny, :] + jnp.where((sub == 7) & has_yh, high, 0.0)
         value = jnp.concatenate([low, high], axis=0)
@@ -337,12 +366,13 @@
             sx = -1 if i == 0 else 1
             there = has_xl if i == 0 else has_xh
             known = ((row == 0) & has_yl) | ((row == ny - 1) & has_yh)
-            face, corner = xs[side, f], cs[side, f]
             if more:
                 top = X_UP if sx > 0 else X_DOWN
-                face = face + extra[top:top + 16]
                 below, above = corner_row(sx, -1), corner_row(sx, 1)
-                corner = corner + jnp.where(row == 0, extra[below:below + 1], extra[above:above + 1])
+                face = extra[top:top + 16]
+                corner = jnp.where(row == 0, extra[below:below + 1], extra[above:above + 1])
+            else:
+                face, corner = xs[side, f], cs[side, f]
             value = value + jnp.where(there, face + jnp.where(known, corner, 0.0), 0.0)
         return value
 
@@ -369,18 +399,47 @@
     lane_p = lax.broadcasted_iota(jnp.int32, (POINTS, nz), 1) % 8
     row_p = lax.broadcasted_iota(jnp.int32, (POINTS, nz), 0)
 
-    def fold_points(value):
+    def fold_points(value, dst):
         up = pltpu.roll(value, nz - 1, 1)
         down = pltpu.roll(value, 1, 1)
         value = value + jnp.where(lane_p == 7, up, 0.0) + jnp.where(lane_p == 0, down, 0.0)
         up = pltpu.roll(value, POINTS - 1, 0)
         down = pltpu.roll(value, 1, 0)
         on_face = row_p < CORNERS
-        extra[...] = (
+        dst[...] = (
             value
             + jnp.where(on_face & (row_p % 16 == 7), up, 0.0)
             + jnp.where(on_face & (row_p % 16 == 8), down, 0.0)
         )
+
+    def gather(src, dst):
+        dst[X_UP:X_UP + 16, :] = src[nx - 1]
+        dst[X_DOWN:X_DOWN + 16, :] = src[0]
+        for i in range(nx):
+            dst[Y_UP + i:Y_UP + i + 1, :] = src[i, ny - 1:ny, :]
+            dst[Y_DOWN + i:Y_DOWN + i + 1, :] = src[i, 0:1, :]
+        for sx in (1, -1):
+            for sy in (1, -1):
+                at, y = corner_row(sx, sy), (ny - 1 if sy > 0 else 0)
+                dst[at:at + 1, :] = src[nx - 1 if sx > 0 else 0, y:y + 1, :]
+
+    def point_copies(pair, e):
+        made = []
+        for n, (ds, dv) in enumerate(SIDES):
+            if dv == 0:
+                a, b, size = (X_UP, X_DOWN, 16) if ds > 0 else (X_DOWN, X_UP, 16)
+            elif ds == 0:
+                a, b, size = (Y_UP, Y_DOWN, 16) if dv > 0 else (Y_DOWN, Y_UP, 16)
+            else:
+                a, b, size = corner_row(ds, dv), corner_row(-ds, -dv), 1
+            made.append([
+                pltpu.make_async_remote_copy(
+                    src_ref=outbox.at[pair, pl.ds(a, size), :], dst_ref=inbox.at[pair, pl.ds(b, size), :],
+                    send_sem=send_sem.at[e, n], recv_sem=recv_sem.at[e, n],
+                    device_id=near(ds, dv), device_id_type=MESH,
+                )
+            ])
+        return launch(made)
 
     def operate(value, parts):
         return wts[...].reshape(rows, nz) * (
@@ -444,7 +503,9 @@
         s = s[:, :128] + s[:, 128:]
         tiles[slot:slot + 1, :] = jnp.sum(s, axis=0, keepdims=True)
 
-    _, quad = gll_tables()
+    table, quad = gll_tables()
+    turned = table.T * quad[None, :] / quad[:, None]
+    stiff = turned @ table
     loads[0].wait()
     column = lax.broadcasted_iota(jnp.int32, (ny, nz), 1)
 
@@ -474,6 +535,8 @@
         imass[i] = time_step * value / wts[i]
 
     loads[1].wait()
+    gather(adj.at[2], mine.at[1])
+    gather(imass, mine.at[2])
     for c in range(3):
         parts = split(flat(adj.at[c]))
         both = left(kxy, parts)
@@ -495,19 +558,23 @@
     for c in range(3):
         fold_store(flat(conv.at[c]) * flat(wts), part3.at[c])
     pl.semaphore_wait(barrier, len(partners))
-    sends = [copies(0, part3), strip_copies(0, part3.at[0], part3.at[1], 0, 1)]
+    sends = [copies(0, part3), strip_copies(0, part3.at[0], part3.at[1], True, turned, 0)]
 
     def right_side(fields):
         pair = jnp.concatenate([fields[0], fields[1]], axis=0)
         return flat(wts) * (left(cxy, split(pair)) + right(split(fields[2]), cz))
 
-    for load in loads[3:]:
+    for load in loads[3:6]:
         load.wait()
-    fold_store(
-        right_side([flat(adj.at[c]) + flat(imass) * flat(part3.at[c]) for c in range(3)]),
-        loc.at[0].at[0],
-    )
-    sends += [copies(1, loc.at[0]), reaction_copies()]
+    gather(part3.at[2], mine.at[0])
+    pair = jnp.concatenate([flat(adj.at[c]) + flat(imass) * flat(part3.at[c]) for c in (0, 1)], axis=0)
+    third = mine[1] + mine[2] * mine[0]
+    fold_points(gw[...] * (left(cf, split(pair)) + right(split(third), cz)), outbox.at[0])
+    sends.append(point_copies(0, 1))
+    for load in loads[6:]:
+        load.wait()
+    sends.append(reaction_copies())
+    gather(reac, mine_reac)
 
     arrive(sends[0])
     for c in range(3):
@@ -517,12 +584,10 @@
             ghost_points(0, c, value, i, c, imass[i])
     fold_store(right_side([flat(moved.at[c]) for c in range(3)]), own.at[0])
     arrive(sends[1])
-    for c in (0, 1):
-        for at in range(POINTS, 208, 8):
-            strips[c, at:at + 8, :] = strips[c, at:at + 8, :] * sc[...]
     ghosts = jnp.concatenate([strips[0], strips[1]], axis=0)
-    fold_points(gw[...] * (left(gc, split(ghosts)) + right(split(strips[2, 0:POINTS, :]), cz)))
+    fold_points(gw[...] * (left(gc, split(ghosts)) + right(split(strips[2, 0:POINTS, :]), cz)), extra)
     arrive(sends[2])
+    extra[...] = extra[...] + inbox[0]
     for i in range(nx):
         vec[0, i] = with_halo(1, 0, own, i, True)
 
@@ -530,10 +595,14 @@
     parts = split(v)
     image = operate(v, parts)
     fold_store(image, loc.at[1].at[0])
-    sends += [copies(2, loc.at[1]), strip_copies(1, loc.at[1].at[0], loc.at[1].at[0], 3, 3)]
+    sends += [copies(2, loc.at[1]), strip_copies(1, loc.at[1].at[0], loc.at[1].at[0], False, stiff, 3)]
     first = flat(loc.at[1].at[0])
-    fold_store(operate(first, split(first)), loc.at[2].at[0])
-    sends.append(copies(3, loc.at[2]))
+    gather(loc.at[1].at[0], mine.at[0])
+    points = mine[0]
+    fold_points(
+        gw[...] * (left(bf, split(first)) + right(split(points), bz) + mine_reac[...] * points), outbox.at[1]
+    )
+    sends.append(point_copies(1, 3))
     to_row(v * v * flat(imult), 0)
     to_row(v * image, 1)
     slopes(parts, 0)
@@ -552,11 +621,12 @@
     arrive(sends[5])
     points = strips[3, 0:POINTS, :]
     fold_points(
-        gw[...] * (left(gb, split(strips[3])) + right(split(points), bz) + ghost_reac[...] * points)
+        gw[...] * (left(gb, split(strips[3])) + right(split(points), bz) + ghost_reac[...] * points), extra
     )
     to_row(v * v * flat(imult), 2)
     to_row(v * image, 3)
     arrive(sends[6])
+    extra[...] = extra[...] + inbox[1]
     for i in range(nx):
         vec[2, i] = with_halo(3, 0, own, i, True)
 
@@ -674,14 +744,19 @@
         pltpu.VMEM((4, STRIPS, nz), F32),
         pltpu.VMEM((POINTS, nz), F32),
         pltpu.VMEM((POINTS, nz), F32),
+        pltpu.VMEM((3, POINTS, nz), F32),
+        pltpu.VMEM((POINTS, nz), F32),
+        pltpu.VMEM((2, POINTS, nz), F32),
+        pltpu.VMEM((2, POINTS, nz), F32),
+        pltpu.VMEM((2, 16, nz), F32),
         pltpu.VMEM((8, 128), F32),
         pltpu.VMEM((n_vert, 128), F32),
         pltpu.VMEM((n_stream, 128), F32),
         pltpu.SemaphoreType.DMA((3 + len(consts),)),
         pltpu.SemaphoreType.DMA((7, 8)),
         pltpu.SemaphoreType.DMA((7, 8)),
-        pltpu.SemaphoreType.DMA((2, 16)),
-        pltpu.SemaphoreType.DMA((2, 16)),
+        pltpu.SemaphoreType.DMA((2, 8)),
+        pltpu.SemaphoreType.DMA((2, 8)),
         pltpu.SemaphoreType.DMA((2,)),
         pltpu.SemaphoreType.DMA((2,)),
     ]

time: 36.3 us -> 35.3 us (0.972)
  Pallas kernels: 35.5 us -> 34.6 us
    pallas_call x1, Pallas kernels: 34.5 us -> 33.5 us  [on_device(): pl.pallas_call(functools.partial(kernel, n_stream, n_vert), out_shape=(pl...]
where the time goes in v6:
time: 35.3 us; the launch traced here: 35.2 us
  Pallas kernels  34.6 us (98%)
  between operations  0.64 us (2%)
    pallas_call x1, Pallas kernels, on_device(): pl.pallas_call(functools.partial(kernel, n_stream, n_vert), out_shape=(pl...  33.5 us
    pallas_call x1, Pallas kernels, on_device(): pl.pallas_call(combine, out_shape=(pltpu.HBM(base_flow.shape, F32), pltpu...  1.04 us

profile of v6, /device:TPU:1, one launch (start us, length us, event | category | flops | bytes accessed | tf_op | source)
XLA Modules:
  0.0 35.2 jit_solution(8858436508086464487)
XLA Ops:
  0.6 33.5 %shard_map.140 = (f32[3,16,16,256]{3,2,1,0:T(8,128)S(1)}, f32[3,3,16,16,256]{4,3,2,1,0:T(8,128)S(1)}, f32[3,16,16,256]{3,2,1,0:T(8,128)S(1)}, f32[8,256]{1,0:T(8,128)S(1)}) custom-call(f32[3,16,16,256]{3,2,1,0:T(8,128)} %base_h.1, f32[3,16,16,256]{3,2,1,0:T(8,128)} %adj_h.1, f32[16,16,256]{2,1,0:T(8,128)} %reac_h.1, f32[48,256]{1,0:T(8,128)} %constant.20.clone.tab_h, ...), custom_call_target="tpu_custom_call" | custom-call | tf_op jit(solution)/shard_map/pallas_call | solution.py:769
  34.2 1.0 %shard_map.141 = (f32[3,16,16,256]{3,2,1,0:T(8,128)}, f32[16,16,256]{2,1,0:T(8,128)}) custom-call(f32[3,16,16,256]{3,2,1,0:T(8,128)S(1)} %get-tuple-element.6.moved, f32[3,3,16,16,256]{4,3,2,1,0:T(8,128)S(1)} %get-tuple-element.7.asm, f32[3,16,16,256]{3,2,1,0:T(8,128)S(1)} %get-tuple-element.8.vec, f32[8,256]{1,0:T(8,128)S(1)} %get-tuple-element.9.coef), custom_call_target="tpu_custom_call" | custom-call | tf_op jit(solution)/shard_map/pallas_call | solution.py:784

commit v7 on v6

--- a/solution.py
+++ b/solution.py
@@ -154,12 +154,18 @@
 
 def left(matrix, parts):
     high, low = parts
-    return dot(matrix[0], high) + dot(matrix[0], low) + dot(matrix[1], high)
+    return dot(
+        jnp.concatenate([matrix[0], matrix[0], matrix[1]], axis=1),
+        jnp.concatenate([high, low, high], axis=0),
+    )
 
 
 def right(parts, matrix):
     high, low = parts
-    return dot(high, matrix[0]) + dot(low, matrix[0]) + dot(high, matrix[1])
+    return dot(
+        jnp.concatenate([high, low, high], axis=1),
+        jnp.concatenate([matrix[0], matrix[0], matrix[1]], axis=0),
+    )
 
 
 def kernel(
@@ -673,6 +679,9 @@
     average(4, 0, 1)
     average(4, 1, 2)
 
+    for made in sends:
+        leave(made)
+    whole(red_a, n_vert, 0).wait_send()
     whole(red_b, n_stream, 1).wait_recv()
     total = jnp.sum(red_b[...], axis=0, keepdims=True)
     m = [jnp.sum(jnp.where(group[0:1] == k, total, 0.0), axis=1, keepdims=True) for k in range(6)]
@@ -698,9 +707,6 @@
     c2 = a2 * f2
     for k, c in enumerate((c0, c1, c2)):
         coef[k:k + 1, :] = jnp.broadcast_to(c, (1, nz))
-    for made in sends:
-        leave(made)
-    whole(red_a, n_vert, 0).wait_send()
     whole(red_b, n_stream, 1).wait_send()
 
 

time: 35.3 us -> 34.9 us (0.989)
  Pallas kernels: 34.6 us -> 34.2 us
    pallas_call x1, Pallas kernels: 33.5 us -> 33.1 us  [on_device(): pl.pallas_call(functools.partial(kernel, n_stream, n_vert), out_shape=(pl...]
where the time goes in v7:
time: 34.9 us; the launch traced here: 34.8 us
  Pallas kernels  34.2 us (98%)
  between operations  0.64 us (2%)
    pallas_call x1, Pallas kernels, on_device(): pl.pallas_call(functools.partial(kernel, n_stream, n_vert), out_shape=(pl...  33.1 us
    pallas_call x1, Pallas kernels, on_device(): pl.pallas_call(combine, out_shape=(pltpu.HBM(base_flow.shape, F32), pltpu...  1.04 us

profile of v7, /device:TPU:1, one launch (start us, length us, event | category | flops | bytes accessed | tf_op | source)
XLA Modules:
  0.0 34.8 jit_solution(12215120717370668151)
XLA Ops:
  0.6 33.1 %shard_map.140 = (f32[3,16,16,256]{3,2,1,0:T(8,128)S(1)}, f32[3,3,16,16,256]{4,3,2,1,0:T(8,128)S(1)}, f32[3,16,16,256]{3,2,1,0:T(8,128)S(1)}, f32[8,256]{1,0:T(8,128)S(1)}) custom-call(f32[3,16,16,256]{3,2,1,0:T(8,128)} %base_h.1, f32[3,16,16,256]{3,2,1,0:T(8,128)} %adj_h.1, f32[16,16,256]{2,1,0:T(8,128)} %reac_h.1, f32[48,256]{1,0:T(8,128)} %constant.20.clone.tab_h, ...), custom_call_target="tpu_custom_call" | custom-call | tf_op jit(solution)/shard_map/pallas_call | solution.py:775
  33.8 1.0 %shard_map.141 = (f32[3,16,16,256]{3,2,1,0:T(8,128)}, f32[16,16,256]{2,1,0:T(8,128)}) custom-call(f32[3,16,16,256]{3,2,1,0:T(8,128)S(1)} %get-tuple-element.6.moved, f32[3,3,16,16,256]{4,3,2,1,0:T(8,128)S(1)} %get-tuple-element.7.asm, f32[3,16,16,256]{3,2,1,0:T(8,128)S(1)} %get-tuple-element.8.vec, f32[8,256]{1,0:T(8,128)S(1)} %get-tuple-element.9.coef), custom_call_target="tpu_custom_call" | custom-call | tf_op jit(solution)/shard_map/pallas_call | solution.py:790

commit v8 on v7

--- a/solution.py
+++ b/solution.py
@@ -564,7 +564,7 @@
     for c in range(3):
         fold_store(flat(conv.at[c]) * flat(wts), part3.at[c])
     pl.semaphore_wait(barrier, len(partners))
-    sends = [copies(0, part3), strip_copies(0, part3.at[0], part3.at[1], True, turned, 0)]
+    sends = [copies(0, part3)]
 
     def right_side(fields):
         pair = jnp.concatenate([fields[0], fields[1]], axis=0)
@@ -576,7 +576,8 @@
     pair = jnp.concatenate([flat(adj.at[c]) + flat(imass) * flat(part3.at[c]) for c in (0, 1)], axis=0)
     third = mine[1] + mine[2] * mine[0]
     fold_points(gw[...] * (left(cf, split(pair)) + right(split(third), cz)), outbox.at[0])
-    sends.append(point_copies(0, 1))
+    ahead = point_copies(0, 1)
+    sends += [strip_copies(0, part3.at[0], part3.at[1], True, turned, 0), ahead]
     for load in loads[6:]:
         load.wait()
     sends.append(reaction_copies())
@@ -601,14 +602,15 @@
     parts = split(v)
     image = operate(v, parts)
     fold_store(image, loc.at[1].at[0])
-    sends += [copies(2, loc.at[1]), strip_copies(1, loc.at[1].at[0], loc.at[1].at[0], False, stiff, 3)]
+    sends.append(copies(2, loc.at[1]))
     first = flat(loc.at[1].at[0])
     gather(loc.at[1].at[0], mine.at[0])
     points = mine[0]
     fold_points(
         gw[...] * (left(bf, split(first)) + right(split(points), bz) + mine_reac[...] * points), outbox.at[1]
     )
-    sends.append(point_copies(1, 3))
+    ahead = point_copies(1, 3)
+    sends += [strip_copies(1, loc.at[1].at[0], loc.at[1].at[0], False, stiff, 3), ahead]
     to_row(v * v * flat(imult), 0)
     to_row(v * image, 1)
     slopes(parts, 0)

time: 34.9 us -> 34.8 us (level)
  no operation moved by 1% of the time
where the time goes in v8:
time: 34.8 us; the launch traced here: 34.7 us
  Pallas kernels  34.1 us (98%)
  between operations  0.64 us (2%)
    pallas_call x1, Pallas kernels, on_device(): pl.pallas_call(functools.partial(kernel, n_stream, n_vert), out_shape=(pl...  33 us
    pallas_call x1, Pallas kernels, on_device(): pl.pallas_call(combine, out_shape=(pltpu.HBM(base_flow.shape, F32), pltpu...  1.04 us

profile of v8, /device:TPU:1, one launch (start us, length us, event | category | flops | bytes accessed | tf_op | source)
XLA Modules:
  0.0 34.7 jit_solution(14033537244048256616)
XLA Ops:
  0.6 33.0 %shard_map.140 = (f32[3,16,16,256]{3,2,1,0:T(8,128)S(1)}, f32[3,3,16,16,256]{4,3,2,1,0:T(8,128)S(1)}, f32[3,16,16,256]{3,2,1,0:T(8,128)S(1)}, f32[8,256]{1,0:T(8,128)S(1)}) custom-call(f32[3,16,16,256]{3,2,1,0:T(8,128)} %base_h.1, f32[3,16,16,256]{3,2,1,0:T(8,128)} %adj_h.1, f32[16,16,256]{2,1,0:T(8,128)} %reac_h.1, f32[48,256]{1,0:T(8,128)} %constant.20.clone.tab_h, ...), custom_call_target="tpu_custom_call" | custom-call | tf_op jit(solution)/shard_map/pallas_call | solution.py:777
  33.7 1.0 %shard_map.141 = (f32[3,16,16,256]{3,2,1,0:T(8,128)}, f32[16,16,256]{2,1,0:T(8,128)}) custom-call(f32[3,16,16,256]{3,2,1,0:T(8,128)S(1)} %get-tuple-element.6.moved, f32[3,3,16,16,256]{4,3,2,1,0:T(8,128)S(1)} %get-tuple-element.7.asm, f32[3,16,16,256]{3,2,1,0:T(8,128)S(1)} %get-tuple-element.8.vec, f32[8,256]{1,0:T(8,128)S(1)} %get-tuple-element.9.coef), custom_call_target="tpu_custom_call" | custom-call | tf_op jit(solution)/shard_map/pallas_call | solution.py:792
